TPU v7x, 256 devices: a whole 4x4x8 slice. The times are simulated.
256 devices in a mesh: member: 16 (over y, x_lo, core), tp: 16 (over x_hi, z).
Axes of the slice: x: 4 (x_hi: 2, x_lo: 2; x = x_hi * 2 + x_lo), y: 4, z: 8, core: 2. Of those that a mesh axis runs over, the one named last changes fastest.
Arguments:
- source: int32 [16], replicated, may hold values from 0 to 15, as said below
- query_rows: bfloat16 [16, 1024, 4096], P('member', None, 'tp'), may hold values from -6 to 6
- key_rows: bfloat16 [16, 1024, 4096], P('member', None, 'tp'), may hold values from -6 to 6
- value_rows: bfloat16 [16, 1024, 4096], P('member', None, 'tp'), may hold values from -6 to 6
- cotangent: bfloat16 [16, 1024, 2560], P('member', 'tp'), may hold values from -6 to 6
- out_weight: bfloat16 [16, 4096, 2560], P('member', 'tp'), may hold values from -0.09375 to 0.09375
- first_moment: bfloat16 [16, 4096, 2560], P('member', 'tp'), may hold values from -24 to 24
- second_moment: bfloat16 [16, 4096, 2560], P('member', 'tp'), may hold values from 4 to 100
Outputs:
- mixture: bfloat16 [16, 1024, 2560], P('member', 'tp')
- query_grad: bfloat16 [16, 1024, 4096], P('member', None, 'tp')
- key_grad: bfloat16 [16, 1024, 4096], P('member', None, 'tp')
- value_grad: bfloat16 [16, 1024, 4096], P('member', None, 'tp')
- new_weight: bfloat16 [16, 4096, 2560], P('member', 'tp')
- new_first: bfloat16 [16, 4096, 2560], P('member', 'tp')
- new_second: bfloat16 [16, 4096, 2560], P('member', 'tp')
Inputs may be any that keep to these rules, and one draw needn't show every extreme that they name: `source`: each entry is the member's own index or the index of one of 4 donor members, which keep their own; 4 members take another's.
All inputs are finite; a program needn't handle non-finite values.
Results may differ from a plain program's by a relative error of at most 0.0096.
Values may be sent and summed in bfloat16 or wider, within the bound.
No kernel may reach another device: no remote copies, remote signals or barrier semaphores. Data moves between devices by JAX's collectives and lax.ppermute only.
A program may use at most 192 MiB of HBM per device.

v0:
```python
import jax
import jax.numpy as jnp
from jax import lax
from jax.sharding import PartitionSpec as P

HD = 128
ADAM_STEP = 100


def attend(query_rows, key_rows, value_rows):
    length = query_rows.shape[0]
    head_count = query_rows.shape[1] // HD
    query_heads = query_rows.reshape(length, head_count, HD)
    key_heads = key_rows.reshape(length, head_count, HD)
    value_heads = value_rows.reshape(length, head_count, HD)
    scores = jnp.einsum(
        "qhd,khd->hqk", query_heads, key_heads, preferred_element_type=jnp.float32
    ) * HD ** (-0.5)
    positions = jnp.arange(length)
    causal = positions[:, None] >= positions[None, :]
    scores = jnp.where(causal[None], scores, -1e30)
    row_max = jnp.max(scores, axis=-1, keepdims=True)
    lifted = jnp.exp(scores - row_max)
    chances = lifted / jnp.sum(lifted, axis=-1, keepdims=True)
    rounded = chances.astype(jnp.bfloat16)
    attended = jnp.einsum("hqk,khd->qhd", rounded, value_heads, preferred_element_type=jnp.float32)
    attended = attended.reshape(length, head_count * HD).astype(jnp.bfloat16)
    return (attended, chances, rounded)


def attend_back(query_rows, key_rows, value_rows, chances, rounded, upstream):
    length = query_rows.shape[0]
    head_count = query_rows.shape[1] // HD
    query_heads = query_rows.reshape(length, head_count, HD)
    key_heads = key_rows.reshape(length, head_count, HD)
    value_heads = value_rows.reshape(length, head_count, HD)
    upstream_heads = upstream.reshape(length, head_count, HD)
    prob_grad = jnp.einsum(
        "qhd,khd->hqk", upstream_heads, value_heads, preferred_element_type=jnp.float32
    )
    value_grad = jnp.einsum(
        "hqk,qhd->khd", rounded, upstream_heads, preferred_element_type=jnp.float32
    )
    center = jnp.sum(chances * prob_grad, axis=-1, keepdims=True)
    score_grad = (chances * (prob_grad - center) * HD ** (-0.5)).astype(jnp.bfloat16)
    query_grad = jnp.einsum(
        "hqk,khd->qhd", score_grad, key_heads, preferred_element_type=jnp.float32
    )
    key_grad = jnp.einsum(
        "hqk,qhd->khd", score_grad, query_heads, preferred_element_type=jnp.float32
    )
    width = head_count * HD
    return (
        query_grad.reshape(length, width).astype(jnp.bfloat16),
        key_grad.reshape(length, width).astype(jnp.bfloat16),
        value_grad.reshape(length, width).astype(jnp.bfloat16),
    )


def adam(weight, moment_one, moment_two, gradient):
    first_full = 0.9 * moment_one.astype(jnp.float32) + 0.1 * gradient
    second_full = 0.999 * moment_two.astype(jnp.float32) + 0.001 * gradient * gradient
    fix_one = 1.0 - 0.9**ADAM_STEP
    fix_two = 1.0 - 0.999**ADAM_STEP
    update = first_full / fix_one / (jnp.sqrt(second_full / fix_two) + 1e-08)
    new_weight = (weight.astype(jnp.float32) - 0.001 * update).astype(jnp.bfloat16)
    return (new_weight, first_full.astype(jnp.bfloat16), second_full.astype(jnp.bfloat16))


def on_device(
    source, query_rows, key_rows, value_rows, cotangent, out_weight, first_moment, second_moment
):
    local_shape = out_weight.shape[1:]
    member_count = lax.axis_size("member")
    flat_weight = out_weight.reshape(member_count, -1)
    flat_first = first_moment.reshape(member_count, -1)
    flat_second = second_moment.reshape(member_count, -1)
    weight = lax.all_to_all(
        jnp.take(
            lax.all_to_all(flat_weight, "member", split_axis=0, concat_axis=0, tiled=True),
            source,
            axis=0,
        ),
        "member",
        split_axis=0,
        concat_axis=0,
        tiled=True,
    ).reshape(local_shape)
    moment_one = lax.all_to_all(
        jnp.take(
            lax.all_to_all(flat_first, "member", split_axis=0, concat_axis=0, tiled=True),
            source,
            axis=0,
        ),
        "member",
        split_axis=0,
        concat_axis=0,
        tiled=True,
    ).reshape(local_shape)
    moment_two = lax.all_to_all(
        jnp.take(
            lax.all_to_all(flat_second, "member", split_axis=0, concat_axis=0, tiled=True),
            source,
            axis=0,
        ),
        "member",
        split_axis=0,
        concat_axis=0,
        tiled=True,
    ).reshape(local_shape)
    attended, chances, rounded = attend(query_rows[0], key_rows[0], value_rows[0])
    segment = attended
    mixture = lax.psum_scatter(
        jnp.dot(segment, weight, preferred_element_type=jnp.float32),
        "tp",
        scatter_dimension=0,
        tiled=True,
    ).astype(jnp.bfloat16)
    incoming = lax.all_gather(cotangent[0], "tp", axis=0, tiled=True)
    back_rows = lax.dot_general(
        incoming, weight, (((1,), (1,)), ((), ())), preferred_element_type=jnp.float32
    )
    segment = attended
    gradient_acc = lax.dot_general(
        segment, incoming, (((0,), (0,)), ((), ())), preferred_element_type=jnp.float32
    )
    upstream = back_rows.astype(jnp.bfloat16)
    query_grad, key_grad, value_grad = attend_back(
        query_rows[0], key_rows[0], value_rows[0], chances, rounded, upstream
    )
    new_weight, new_first, new_second = adam(weight, moment_one, moment_two, gradient_acc)
    return (
        mixture[None],
        query_grad[None],
        key_grad[None],
        value_grad[None],
        new_weight[None],
        new_first[None],
        new_second[None],
    )


def solution(mesh):
    placed = (
        P(),
        P("member", None, "tp"),
        P("member", None, "tp"),
        P("member", None, "tp"),
        P("member", "tp", None),
        P("member", "tp", None),
        P("member", "tp", None),
        P("member", "tp", None),
    )
    return jax.shard_map(
        on_device,
        mesh=mesh,
        in_specs=placed,
        out_specs=(
            P("member", "tp", None),
            P("member", None, "tp"),
            P("member", None, "tp"),
            P("member", None, "tp"),
            P("member", "tp", None),
            P("member", "tp", None),
            P("member", "tp", None),
        ),
        check_vma=False,
    )
```

profile of v0, /device:TPU:8, one launch (start us, length us, event | category | flops | bytes accessed | tf_op | source)
XLA Modules:
  0.0 457.9 jit_solution(1774047834345194295)
XLA Ops:
  7.2 4.2 all_to_all.57
  11.3 0.5 broadcast.93
  11.8 9.7 %reduce.7 = bf16[16,40960]{1,0:T(8,128)(2,1)} reduce(bf16[16,1,40960]{2,1,0:T(2,128)(2,1)S(1)} %all_to_all.57, bf16[]{:T(256)} %broadcast.93), dimensions={1}, to_apply=%all_to_all.57.reduce_sub_computation | reduce | bytes 2621442 | tf_op jit(solution)/shard_map/all_to_all | solution.py:80
  21.5 2.9 reshape.147
  24.4 6.9 %all-to-all-start = ((bf16[16,2,20480]{2,1,0:T(2,128)(2,1)}), bf16[16,2,20480]{2,1,0:T(2,128)(2,1)}, u32[]{:S(2)}, u32[]{:S(2)}) async-start(bf16[16,2,20480]{2,1,0:T(2,128)(2,1)} %reshape.147), calls=%async_computation | async-start | bytes 2621440 | tf_op jit(solution)/shard_map/all_to_all | solution.py:80
  31.4 4.2 all_to_all.58
  35.6 9.7 %reduce.6 = bf16[16,40960]{1,0:T(8,128)(2,1)} reduce(bf16[16,1,40960]{2,1,0:T(2,128)(2,1)S(1)} %all_to_all.58, bf16[]{:T(256)} %broadcast.93), dimensions={1}, to_apply=%all_to_all.58.reduce_sub_computation | reduce | bytes 2621442 | tf_op jit(solution)/shard_map/all_to_all | solution.py:91
  45.2 2.9 reshape.151
  48.2 0.5 all-to-all-done
  48.7 6.7 %all-to-all-start.2 = ((bf16[16,2,20480]{2,1,0:T(2,128)(2,1)}), bf16[16,2,20480]{2,1,0:T(2,128)(2,1)}, u32[]{:S(2)}, u32[]{:S(2)}) async-start(bf16[16,2,20480]{2,1,0:T(2,128)(2,1)} %reshape.151), calls=%async_computation.3 | async-start | bytes 2621440 | tf_op jit(solution)/shard_map/all_to_all | solution.py:91
  55.4 4.2 all_to_all.59
  59.6 9.7 %reduce.5 = bf16[16,40960]{1,0:T(8,128)(2,1)} reduce(bf16[16,1,40960]{2,1,0:T(2,128)(2,1)S(1)} %all_to_all.59, bf16[]{:T(256)} %broadcast.93), dimensions={1}, to_apply=%all_to_all.59.reduce_sub_computation | reduce | bytes 2621442 | tf_op jit(solution)/shard_map/all_to_all | solution.py:102
  69.3 3.0 reshape.155
  72.3 0.5 all-to-all-done.2
  72.7 6.4 %all-to-all-start.4 = ((bf16[16,2,20480]{2,1,0:T(2,128)(2,1)}), bf16[16,2,20480]{2,1,0:T(2,128)(2,1)}, u32[]{:S(2)}, u32[]{:S(2)}) async-start(bf16[16,2,20480]{2,1,0:T(2,128)(2,1)} %reshape.155), calls=%async_computation.5 | async-start | bytes 2621440 | tf_op jit(solution)/shard_map/all_to_all | solution.py:102
  80.2 1.0 copy.75
  81.2 1.3 iota_compare_fusion
  82.5 6.1 %reshape.148 = bf16[16,1,40960]{2,1,0:T(2,128)(2,1)} reshape(bf16[16,2,20480]{2,1,0:T(2,128)(2,1)} %all-to-all-done) | data formatting | bytes 2621440
  88.6 3.2 copy.85
  91.7 6.1 %reshape.152 = bf16[16,1,40960]{2,1,0:T(2,128)(2,1)} reshape(bf16[16,2,20480]{2,1,0:T(2,128)(2,1)} %all-to-all-done.2) | data formatting | bytes 2621440
  97.8 3.2 copy.84
  101.0 2.5 gather_fusion
  103.5 2.5 gather_fusion.1
  106.0 6.1 %reshape.156 = bf16[16,1,40960]{2,1,0:T(2,128)(2,1)} reshape(bf16[16,2,20480]{2,1,0:T(2,128)(2,1)} %all-to-all-done.4) | data formatting | bytes 2621440
  112.1 3.2 copy.83
  115.3 2.5 gather_fusion.2
  117.8 3.8 select_bitcast_fusion
  121.6 3.0 reduce.8
  124.6 1.9 reshape.149
  126.5 5.9 %all-to-all-start.1 = ((bf16[16,2,20480]{2,1,0:T(2,128)(2,1)}), bf16[16,2,20480]{2,1,0:T(2,128)(2,1)}, u32[]{:S(2)}, u32[]{:S(2)}) async-start(bf16[16,2,20480]{2,1,0:T(2,128)(2,1)} %reshape.149), calls=%async_computation.1 | async-start | bytes 2621440 | tf_op jit(solution)/shard_map/all_to_all | solution.py:78
  132.8 5.3 %fusion.51 = (f32[2,1024]{1,0:T(2,128)S(1)}, f32[2,1024,1024]{1,2,0:T(8,128)}) fusion(pred[1024,1024]{0,1:T(8,128)(4,1)S(1)} %copy-done.5, bf16[1024,2,128]{0,2,1:T(8,128)(2,1)S(1)} %bitcast.68, bf16[1024,2,128]{0,2,1:T(8,128)(2,1)S(1)} %bitcast.71), kind=kOutput, calls=%fused_computation.60 | convolution fusion | flops 545260544 | bytes 10493952 | tf_op jit(solution)/shard_map/sub | solution.py:23
  138.3 5.0 %fusion.25 = bf16[2,1024,128]{1,2,0:T(8,128)(2,1)} fusion(bf16[1024,2,128]{2,1,0:T(2,128)(2,1)S(1)} %reshape_squeeze.14, f32[2,1024,1024]{1,2,0:T(8,128)} %get-tuple-element.36, f32[2,1024]{1,0:T(2,128)S(1)} %get-tuple-element.35), kind=kOutput, calls=%fused_computation.41 | convolution fusion | flops 541327360 | bytes 9445376 | tf_op jit(solution)/shard_map/hqk,khd->qhd/dot_general | solution.py:26
  143.3 17.7 %all-to-all-done.1 = bf16[16,2,20480]{2,1,0:T(2,128)(2,1)} async-done(((bf16[16,2,20480]{2,1,0:T(2,128)(2,1)}), bf16[16,2,20480]{2,1,0:T(2,128)(2,1)}, u32[]{:S(2)}, u32[]{:S(2)}) %all-to-all-start.1) | async-done | bytes 1310752 | tf_op jit(solution)/shard_map/all_to_all | solution.py:78
  160.9 4.5 reshape.150
  165.4 9.0 %reduce = bf16[16,40960]{1,0:T(8,128)(2,1)} reduce(bf16[16,1,40960]{2,1,0:T(2,128)(2,1)S(1)} %reshape.150, bf16[]{:T(256)} %constant.41), dimensions={1}, to_apply=%all_to_all.46.reduce_sub_computation | reduce | bytes 2621442 | tf_op jit(solution)/shard_map/all_to_all | solution.py:78
  174.5 1.9 reshape.108
  176.4 5.6 %fusion.54 = f32[1024,2560]{1,0:T(8,128)} fusion(bf16[1024,256]{0,1:T(8,128)(2,1)S(1)} %bitcast.64, bf16[256,2560]{1,0:T(8,128)(2,1)S(1)} %reshape.108), kind=kOutput, calls=%fused_computation.61 | convolution fusion | flops 1342177280 | bytes 12320768 | tf_op jit(solution)/shard_map/dot_general | solution.py:114
  182.0 1.3 copy-done.4
  183.3 1.6 reduce.10
  185.0 1.9 reshape.153
  186.8 6.1 %all-to-all-start.3 = ((bf16[16,2,20480]{2,1,0:T(2,128)(2,1)}), bf16[16,2,20480]{2,1,0:T(2,128)(2,1)S(1)}, u32[]{:S(2)}, u32[]{:S(2)}) async-start(bf16[16,2,20480]{2,1,0:T(2,128)(2,1)} %reshape.153), calls=%async_computation.4 | async-start | bytes 2621440 | tf_op jit(solution)/shard_map/all_to_all | solution.py:89
  193.0 3.0 reduce.9
  195.9 1.9 reshape.157
  197.8 12.5 %all-to-all-done.3 = bf16[16,2,20480]{2,1,0:T(2,128)(2,1)S(1)} async-done(((bf16[16,2,20480]{2,1,0:T(2,128)(2,1)}), bf16[16,2,20480]{2,1,0:T(2,128)(2,1)S(1)}, u32[]{:S(2)}, u32[]{:S(2)}) %all-to-all-start.3) | async-done | bytes 1310752 | tf_op jit(solution)/shard_map/all_to_all | solution.py:89
  210.3 1.1 copy-done.3
  211.4 6.4 %all-to-all-start.5 = ((bf16[16,2,20480]{2,1,0:T(2,128)(2,1)}), bf16[16,2,20480]{2,1,0:T(2,128)(2,1)}, u32[]{:S(2)}, u32[]{:S(2)}) async-start(bf16[16,2,20480]{2,1,0:T(2,128)(2,1)} %reshape.157), calls=%async_computation.6 | async-start | bytes 2621440 | tf_op jit(solution)/shard_map/all_to_all | solution.py:100
  217.8 4.5 reshape.154
  222.3 9.7 %multiply_reduce_fusion.2 = f32[16,40960]{1,0:T(8,128)} fusion(bf16[16,1,40960]{2,1,0:T(2,128)(2,1)S(1)} %reshape.154), kind=kLoop, calls=%fused_computation.27 | loop fusion | flops 1310720 | bytes 3932160 | tf_op jit(solution)/shard_map/mul | solution.py:61
  232.0 3.0 mul.51
  235.1 6.2 %all-to-all-done.5 = bf16[16,2,20480]{2,1,0:T(2,128)(2,1)} async-done(((bf16[16,2,20480]{2,1,0:T(2,128)(2,1)}), bf16[16,2,20480]{2,1,0:T(2,128)(2,1)}, u32[]{:S(2)}, u32[]{:S(2)}) %all-to-all-start.5) | async-done | bytes 1310752 | tf_op jit(solution)/shard_map/all_to_all | solution.py:100
  241.3 4.7 %reshape.158 = bf16[16,1,40960]{2,1,0:T(2,128)(2,1)S(1)} reshape(bf16[16,2,20480]{2,1,0:T(2,128)(2,1)} %all-to-all-done.5) | data formatting | bytes 2621440
  246.0 9.7 %multiply_reduce_fusion.1 = f32[16,40960]{1,0:T(8,128)} fusion(bf16[16,1,40960]{2,1,0:T(2,128)(2,1)S(1)} %reshape.158), kind=kLoop, calls=%fused_computation.25 | loop fusion | flops 1310720 | bytes 3932160 | tf_op jit(solution)/shard_map/mul | solution.py:62
  255.7 3.4 mul.56
  259.2 4.4 fusion.31
  263.5 4.6 %fusion.43 = f32[2,1024,1024]{1,2,0:T(8,128)} fusion(bf16[1024,2,128]{0,2,1:T(8,128)(2,1)S(1)} %bitcast.66, bf16[1024,2,128]{2,1,0:T(2,128)(2,1)S(1)} %reshape_squeeze.14), kind=kOutput, calls=%fused_computation.48 | convolution fusion | flops 536870912 | bytes 9437184 | tf_op jit(solution)/shard_map/qhd,khd->hqk/dot_general | solution.py:38
  268.1 14.1 %fusion.34 = bf16[2,1024,128]{1,2,0:T(8,128)(2,1)S(1)} fusion(bf16[1024,2,128]{0,2,1:T(8,128)(2,1)} %bitcast.70, f32[2,1024,1024]{1,2,0:T(8,128)} %fusion.43, f32[2,1024,1024]{1,2,0:T(8,128)} %get-tuple-element.36, f32[2,1024]{1,0:T(2,128)S(1)} %get-tuple-element.35), kind=kOutput, calls=%fused_computation.44 | convolution fusion | flops 551816192 | bytes 17833984 | tf_op jit(solution)/shard_map/hqk,khd->qhd/dot_general | solution.py:46
  282.2 1.0 copy.63
  283.2 12.8 %fusion.37 = bf16[2,1024,128]{1,2,0:T(8,128)(2,1)S(1)} fusion(bf16[1024,2,128]{0,2,1:T(8,128)(2,1)S(1)} %bitcast.69, f32[2,1024,1024]{1,2,0:T(8,128)} %fusion.43, f32[2,1024,1024]{1,2,0:T(8,128)} %get-tuple-element.36, f32[2,1024]{1,0:T(2,128)S(1)} %get-tuple-element.35), kind=kOutput, calls=%fused_computation.45 | convolution fusion | flops 551816192 | bytes 17833984 | tf_op jit(solution)/shard_map/hqk,qhd->khd/dot_general | solution.py:49
  296.1 1.0 copy.64
  297.1 5.0 %fusion.28 = bf16[2,128,1024]{2,1,0:T(8,128)(2,1)S(1)} fusion(bf16[1024,2,128]{0,2,1:T(8,128)(2,1)S(1)} %bitcast.67, f32[2,1024,1024]{1,2,0:T(8,128)} %get-tuple-element.36, f32[2,1024]{1,0:T(2,128)S(1)} %get-tuple-element.35), kind=kOutput, calls=%fused_computation.42 | convolution fusion | flops 541327360 | bytes 9445376 | tf_op jit(solution)/shard_map/hqk,qhd->khd/dot_general | solution.py:41
  302.1 1.0 copy.65
  303.1 8.9 %convert_bitcast_fusion = (bf16[1,256,2560]{2,1,0:T(8,128)(2,1)}, bf16[1,256,2560]{2,1,0:T(8,128)(2,1)}, bf16[1,256,2560]{2,1,0:T(8,128)(2,1)}) fusion(f32[256,2560]{1,0:T(8,128)} %mul.56, f32[256,2560]{1,0:T(8,128)} %mul.51, bf16[256,2560]{1,0:T(8,128)(2,1)S(1)} %copy-done.1, bf16[1024,256]{0,1:T(8,128)(2,1)S(1)} %bitcast.65, ...), kind=kOutput, calls=%fused_computation.38 | convolution fusion | flops 1352007680 | bytes 16252928 | tf_op jit(solution)/shard_map/dot_general | solution.py:124
  312.0 136.7 %reduce-scatter.2.cloned.1.call-done = f32[64,2560]{1,0:T(8,128)} async-done(((f32[1024,2560]{1,0:T(8,128)}), f32[64,2560]{1,0:T(8,128)}) %reduce-scatter.2.cloned.1.call-update) | async-done | bytes 655376 | tf_op jit(solution)/shard_map/reduce_scatter | solution.py:113
  448.7 1.8 convert_bitcast_fusion.2
  (39 shorter events, 1.6 us)
Async XLA Ops:
  24.4 24.3 %all-to-all-start = ((bf16[16,2,20480]{2,1,0:T(2,128)(2,1)}), bf16[16,2,20480]{2,1,0:T(2,128)(2,1)}, u32[]{:S(2)}, u32[]{:S(2)}) async-start(bf16[16,2,20480]{2,1,0:T(2,128)(2,1)} %reshape.147), calls=%async_computation | async-start | bytes 2621440 | tf_op jit(solution)/shard_map/all_to_all | solution.py:80
  48.7 24.1 %all-to-all-start.2 = ((bf16[16,2,20480]{2,1,0:T(2,128)(2,1)}), bf16[16,2,20480]{2,1,0:T(2,128)(2,1)}, u32[]{:S(2)}, u32[]{:S(2)}) async-start(bf16[16,2,20480]{2,1,0:T(2,128)(2,1)} %reshape.151), calls=%async_computation.3 | async-start | bytes 2621440 | tf_op jit(solution)/shard_map/all_to_all | solution.py:91
  69.3 10.6 %copy-start.8 = (bf16[1,1024,256]{2,1,0:T(8,128)(2,1)S(1)}, bf16[1,1024,256]{2,1,0:T(8,128)(2,1)}, u32[]{:S(2)}) copy-start(bf16[1,1024,256]{2,1,0:T(8,128)(2,1)} %param.11) | copy-start | bytes 1572868
  72.3 7.9 %copy-start.9 = (bf16[1,1024,256]{2,1,0:T(8,128)(2,1)S(1)}, bf16[1,1024,256]{2,1,0:T(8,128)(2,1)}, u32[]{:S(2)}) copy-start(bf16[1,1024,256]{2,1,0:T(8,128)(2,1)} %param.12) | copy-start | bytes 1572868
  72.3 8.9 %copy-start.14 = (s32[16]{0:T(128)S(1)}, s32[16]{0:T(128)}, u32[]{:S(2)}) copy-start(s32[16]{0:T(128)} %param.10) | copy-start | bytes 196
  72.7 33.3 %all-to-all-start.4 = ((bf16[16,2,20480]{2,1,0:T(2,128)(2,1)}), bf16[16,2,20480]{2,1,0:T(2,128)(2,1)}, u32[]{:S(2)}, u32[]{:S(2)}) async-start(bf16[16,2,20480]{2,1,0:T(2,128)(2,1)} %reshape.155), calls=%async_computation.5 | async-start | bytes 2621440 | tf_op jit(solution)/shard_map/all_to_all | solution.py:102
  79.2 180.0 %all-gather.3.cloned.1.call-start = ((), (), s32[]{:S(2)}) async-start(), calls=%async_computation.8 | async-start | bytes 5570560 | tf_op jit(solution)/shard_map/all_gather | solution.py:119
  80.1 52.6 %copy-start.11 = (bf16[1,1024,256]{1,2,0:T(8,128)(2,1)}, bf16[1,1024,256]{1,2,0:T(8,128)(2,1)S(1)}, u32[]{:S(2)}) copy-start(bf16[1,1024,256]{1,2,0:T(8,128)(2,1)S(1)} %copy.74) | copy-start | bytes 1572868
  115.3 2.5 copy-start.2
  124.6 8.2 %copy-start.5 = (pred[1024,1024]{0,1:T(8,128)(4,1)S(1)}, pred[1024,1024]{0,1:T(8,128)(4,1)}, u32[]{:S(2)}) copy-start(pred[1024,1024]{0,1:T(8,128)(4,1)} %iota_compare_fusion) | copy-start | bytes 3145732
  126.5 6.4 %copy-start.13 = (bf16[1,1024,256]{1,2,0:T(8,128)(2,1)S(1)}, bf16[1,1024,256]{1,2,0:T(8,128)(2,1)}, u32[]{:S(2)}) copy-start(bf16[1,1024,256]{1,2,0:T(8,128)(2,1)} %copy.75) | copy-start | bytes 1572868
  126.5 34.5 %all-to-all-start.1 = ((bf16[16,2,20480]{2,1,0:T(2,128)(2,1)}), bf16[16,2,20480]{2,1,0:T(2,128)(2,1)}, u32[]{:S(2)}, u32[]{:S(2)}) async-start(bf16[16,2,20480]{2,1,0:T(2,128)(2,1)} %reshape.149), calls=%async_computation.1 | async-start | bytes 2621440 | tf_op jit(solution)/shard_map/all_to_all | solution.py:78
  132.3 316.4 %reduce-scatter.2.cloned.1.call-start = ((), (), s32[]{:S(2)}) async-start(), calls=%async_computation.7 | async-start | bytes 11141120 | tf_op jit(solution)/shard_map/reduce_scatter | solution.py:113
  132.8 5.3 %copy-start.10 = (bf16[1,1024,256]{2,1,0:T(8,128)(2,1)S(1)}, bf16[1,1024,256]{2,1,0:T(8,128)(2,1)}, u32[]{:S(2)}) copy-start(bf16[1,1024,256]{2,1,0:T(8,128)(2,1)} %param.13) | copy-start | bytes 1572868
  174.5 2.0 copy-start.6
  176.4 5.6 %copy-start = (bf16[256,2560]{1,0:T(8,128)(2,1)}, bf16[256,2560]{1,0:T(8,128)(2,1)S(1)}, u32[]{:S(2)}) copy-start(bf16[256,2560]{1,0:T(8,128)(2,1)S(1)} %reshape.108) | copy-start | bytes 3932164
  182.0 1.3 copy-start.4
  186.8 23.5 %all-to-all-start.3 = ((bf16[16,2,20480]{2,1,0:T(2,128)(2,1)}), bf16[16,2,20480]{2,1,0:T(2,128)(2,1)S(1)}, u32[]{:S(2)}, u32[]{:S(2)}) async-start(bf16[16,2,20480]{2,1,0:T(2,128)(2,1)} %reshape.153), calls=%async_computation.4 | async-start | bytes 2621440 | tf_op jit(solution)/shard_map/all_to_all | solution.py:89
  210.3 1.1 copy-start.3
  211.4 29.9 %all-to-all-start.5 = ((bf16[16,2,20480]{2,1,0:T(2,128)(2,1)}), bf16[16,2,20480]{2,1,0:T(2,128)(2,1)}, u32[]{:S(2)}, u32[]{:S(2)}) async-start(bf16[16,2,20480]{2,1,0:T(2,128)(2,1)} %reshape.157), calls=%async_computation.6 | async-start | bytes 2621440 | tf_op jit(solution)/shard_map/all_to_all | solution.py:100
  255.7 3.5 copy-start.1
  268.1 15.1 %copy-start.12 = (bf16[1,1024,256]{1,2,0:T(8,128)(2,1)S(1)}, bf16[1,1024,256]{1,2,0:T(8,128)(2,1)}, u32[]{:S(2)}) copy-start(bf16[1,1024,256]{1,2,0:T(8,128)(2,1)} %copy-done.11) | copy-start | bytes 1572868
  297.1 6.0 %copy-start.7 = (bf16[2,1024,128]{1,2,0:T(8,128)(2,1)S(1)}, bf16[2,1024,128]{1,2,0:T(8,128)(2,1)}, u32[]{:S(2)}) copy-start(bf16[2,1024,128]{1,2,0:T(8,128)(2,1)} %fusion.25) | copy-start | bytes 1572868
Sparse Core Ops, SparseCore 0:
  82.6 122.0 all-gather.2
  208.8 239.8 reduce-scatter.1
where the time goes:
time: 466 us; the launch traced here: 458 us
  waiting for transfers between devices  175 us (38%)
  local copies, waits for them, and re-layouts  91.6 us (20%)
  other arithmetic  72 us (15%)
  matrix products  65.6 us (14%)
  starting transfers between devices  39.3 us (8%)
  between operations  14.7 us (3%)
    reduce_scatter x1, waiting for transfers between devices, on_device(): lax.psum_scatter(jnp.dot(segment, weight, preferred_element_type=jnp.floa...  137 us
    unnamed x48, local copies, waits for them, and re-layouts  61.5 us
    all_to_all x1, waiting for transfers between devices, on_device(): lax.all_to_all(jnp.take(lax.all_to_all(flat_weight, 'member', split_axis=...  17.7 us
    dot_general x1, matrix products, attend_back(): jnp.einsum('hqk,khd->qhd', score_grad, key_heads, preferred_element_type=...  14.1 us
    dot_general x1, matrix products, attend_back(): jnp.einsum('hqk,qhd->khd', score_grad, query_heads, preferred_element_typ...  12.8 us
    all_to_all x1, waiting for transfers between devices, on_device(): lax.all_to_all(jnp.take(lax.all_to_all(flat_first, 'member', split_axis=0...  12.5 us
    all_to_all x2, other arithmetic, on_device(): lax.all_to_all(jnp.take(lax.all_to_all(flat_weight, 'member', split_axis=...  12 us
    mul x1, other arithmetic, adam(): 0.999 * moment_two.astype(jnp.float32) + 0.001 * gradient * gradient  9.69 us
  transfers between devices with their start and end apart: 8, of which 6 were waited for; matrix products, arithmetic and copies ran while one was open for 44% of the time, Pallas kernels for 0%

commit v1 on v0

v1 whole, which is shorter than its diff:
```python
import jax
import jax.numpy as jnp
from jax import lax
from jax.experimental import pallas as pl
from jax.experimental.pallas import tpu as pltpu
from jax.sharding import PartitionSpec as P

HD = 128
ADAM_STEP = 100
MEMBERS = 16
ZED = 8
HALVES = 2
TOK = 1024
DOUT = 2560
COLS = 256
CHUNK = TOK // (ZED * HALVES)
QB = 256
SCALE = HD ** (-0.5)
VMEM_BYTES = 48 * 1024 * 1024

Z_GROUPS = [[half * ZED + z for z in range(ZED)] for half in range(HALVES)]
HALF_SWAP = [(t, (t + ZED) % (ZED * HALVES)) for t in range(ZED * HALVES)]

NN = (((1,), (0,)), ((), ()))
NT = (((1,), (1,)), ((), ()))


def mm(a, b, dims):
    return lax.dot_general(a, b, dims, preferred_element_type=jnp.float32)


def params(**more):
    return pltpu.CompilerParams(vmem_limit_bytes=VMEM_BYTES, **more)


def cost(flops, nbytes, trans=0):
    return pl.CostEstimate(flops=flops, bytes_accessed=nbytes, transcendentals=trans)


def place(t):
    return (t % ZED) * HALVES + t // ZED


def forward_kernel(q_ref, k_ref, v_ref, att_ref, p_ref):
    keys = k_ref[...]
    values_t = v_ref[...].astype(jnp.float32).T.astype(jnp.bfloat16)
    row = lax.broadcasted_iota(jnp.int32, (QB, QB), 0)
    col = lax.broadcasted_iota(jnp.int32, (QB, QB), 1)
    visible = row <= col
    for i in range(TOK // QB):
        low, high = i * QB, (i + 1) * QB
        queries = q_ref[low:high, :]
        last = jnp.where(visible, mm(keys[low:high], queries, NT) * SCALE, -1e30)
        top = jnp.max(last, axis=0, keepdims=True)
        if i:
            early = mm(keys[:low], queries, NT) * SCALE
            top = jnp.maximum(top, jnp.max(early, axis=0, keepdims=True))
            early = jnp.exp(early - top)
        last = jnp.exp(last - top)
        total = jnp.sum(last, axis=0, keepdims=True)
        if i:
            total = total + jnp.sum(early, axis=0, keepdims=True)
        inverse = 1.0 / total
        last = (last * inverse).astype(jnp.bfloat16)
        p_ref[0, low:high, low:high] = last
        out_t = mm(values_t[:, low:high], last, NN)
        if i:
            early = (early * inverse).astype(jnp.bfloat16)
            p_ref[0, :low, low:high] = early
            out_t = out_t + mm(values_t[:, :low], early, NN)
        rows = out_t.T.astype(jnp.bfloat16)
        for part in range(QB // CHUNK):
            att_ref[place(i * (QB // CHUNK) + part)] = rows[part * CHUNK : (part + 1) * CHUNK]


def forward(queries, keys, values):
    heads = COLS // HD
    head_block = pl.BlockSpec((TOK, HD), lambda h: (0, h))
    return pl.pallas_call(
        forward_kernel,
        grid=(heads,),
        in_specs=[head_block] * 3,
        out_specs=[
            pl.BlockSpec((ZED * HALVES, CHUNK, HD), lambda h: (0, 0, h)),
            pl.BlockSpec((1, TOK, TOK), lambda h: (h, 0, 0)),
        ],
        out_shape=[
            jax.ShapeDtypeStruct((ZED * HALVES, CHUNK, COLS), jnp.bfloat16),
            jax.ShapeDtypeStruct((heads, TOK, TOK), jnp.bfloat16),
        ],
        compiler_params=params(),
        cost_estimate=cost(4 * TOK * TOK * COLS, 8 * TOK * COLS + 2 * heads * TOK * TOK, heads * TOK * TOK),
        name="attend_forward",
    )(queries, keys, values)


def project_kernel(a_ref, w_ref, o_ref):
    o_ref[...] = mm(a_ref[...], w_ref[...], NN).astype(jnp.bfloat16)


def project(attended, weight):
    block = 256
    return pl.pallas_call(
        project_kernel,
        grid=(TOK // block,),
        in_specs=[
            pl.BlockSpec((block, COLS), lambda i: (i, 0)),
            pl.BlockSpec((COLS, DOUT), lambda i: (0, 0)),
        ],
        out_specs=pl.BlockSpec((block, DOUT), lambda i: (i, 0)),
        out_shape=jax.ShapeDtypeStruct((TOK, DOUT), jnp.bfloat16),
        compiler_params=params(),
        cost_estimate=cost(2 * TOK * COLS * DOUT, 2 * (TOK * COLS + COLS * DOUT + TOK * DOUT)),
        name="project",
    )(attended, weight)


def gradient_kernel(a_ref, c_ref, o_ref, t_ref):
    @pl.when(pl.program_id(0) == 0)
    def _():
        t_ref[...] = a_ref[...].astype(jnp.float32).T.astype(jnp.bfloat16)

    o_ref[...] = mm(t_ref[...], c_ref[...], NN)


def gradient_of(attended, incoming):
    block = 512
    return pl.pallas_call(
        gradient_kernel,
        grid=(DOUT // block,),
        in_specs=[
            pl.BlockSpec((TOK, COLS), lambda i: (0, 0)),
            pl.BlockSpec((TOK, block), lambda i: (0, i)),
        ],
        out_specs=pl.BlockSpec((COLS, block), lambda i: (0, i)),
        out_shape=jax.ShapeDtypeStruct((COLS, DOUT), jnp.float32),
        scratch_shapes=[pltpu.VMEM((COLS, TOK), jnp.bfloat16)],
        compiler_params=params(),
        cost_estimate=cost(2 * TOK * COLS * DOUT, 2 * TOK * (COLS + DOUT) + 4 * COLS * DOUT),
        name="weight_gradient",
    )(attended, incoming)


def backward_kernel(c_ref, w_ref, q_ref, k_ref, v_ref, p_ref, dq_ref, dk_ref, dv_ref, u_ref, ak_ref, av_ref):
    head = pl.program_id(0)

    @pl.when(head == 0)
    def _():
        step = 256
        for block in range(TOK // step):
            rows = mm(c_ref[block * step : (block + 1) * step, :], w_ref[...], NT).astype(jnp.bfloat16)
            for part in range(step // CHUNK):
                spot = block * (step // CHUNK) + part
                t = (spot % HALVES) * ZED + spot // HALVES
                for h in range(COLS // HD):
                    u_ref[h, t * CHUNK : (t + 1) * CHUNK, :] = rows[
                        part * CHUNK : (part + 1) * CHUNK, h * HD : (h + 1) * HD
                    ]

    keys_t = k_ref[...].astype(jnp.float32).T.astype(jnp.bfloat16)
    blocks = TOK // QB
    for i in reversed(range(blocks)):
        low, high = i * QB, (i + 1) * QB
        up = u_ref[head, low:high, :]
        chance = p_ref[0, :high, low:high]
        wide = chance.astype(jnp.float32)
        prob_grad = mm(v_ref[:high, :], up, NT)
        center = jnp.sum(wide * prob_grad, axis=0, keepdims=True)
        score_grad = (wide * (prob_grad - center) * SCALE).astype(jnp.bfloat16)
        dq_ref[low:high, :] = mm(keys_t[:, :high], score_grad, NN).T.astype(jnp.bfloat16)
        more_v = mm(chance, up, NN)
        more_k = mm(score_grad, q_ref[low:high, :], NN)
        if i == blocks - 1:
            av_ref[...] = more_v
            ak_ref[...] = more_k
        else:
            av_ref[:high, :] += more_v
            ak_ref[:high, :] += more_k
    dv_ref[...] = av_ref[...].astype(jnp.bfloat16)
    dk_ref[...] = ak_ref[...].astype(jnp.bfloat16)


def backward(incoming, weight, queries, keys, values, chances):
    heads = COLS // HD
    head_block = pl.BlockSpec((TOK, HD), lambda h: (0, h))
    return pl.pallas_call(
        backward_kernel,
        grid=(heads,),
        in_specs=[
            pl.BlockSpec((TOK, DOUT), lambda h: (0, 0)),
            pl.BlockSpec((COLS, DOUT), lambda h: (0, 0)),
            head_block,
            head_block,
            head_block,
            pl.BlockSpec((1, TOK, TOK), lambda h: (h, 0, 0)),
        ],
        out_specs=[head_block] * 3,
        out_shape=[jax.ShapeDtypeStruct((TOK, COLS), jnp.bfloat16)] * 3,
        scratch_shapes=[
            pltpu.VMEM((heads, TOK, HD), jnp.bfloat16),
            pltpu.VMEM((TOK, HD), jnp.float32),
            pltpu.VMEM((TOK, HD), jnp.float32),
        ],
        compiler_params=params(),
        cost_estimate=cost(
            2 * TOK * COLS * DOUT + 8 * TOK * TOK * COLS, 2 * (TOK * DOUT + COLS * DOUT + 6 * TOK * COLS + heads * TOK * TOK)
        ),
        name="attend_backward",
    )(incoming, weight, queries, keys, values, chances)


def adam_kernel(w_ref, one_ref, two_ref, g_ref, nw_ref, n1_ref, n2_ref):
    shape = g_ref.shape
    gradient = g_ref[...]
    first_full = 0.9 * one_ref[...].reshape(shape).astype(jnp.float32) + 0.1 * gradient
    second_full = 0.999 * two_ref[...].reshape(shape).astype(jnp.float32) + 0.001 * gradient * gradient
    fix_one = 1.0 - 0.9**ADAM_STEP
    fix_two = 1.0 - 0.999**ADAM_STEP
    update = first_full / fix_one / (jnp.sqrt(second_full / fix_two) + 1e-08)
    nw_ref[...] = (w_ref[...].astype(jnp.float32) - 0.001 * update).astype(jnp.bfloat16)
    n1_ref[...] = first_full.astype(jnp.bfloat16)
    n2_ref[...] = second_full.astype(jnp.bfloat16)


def adam(weight, moments, gradient):
    piece = COLS // MEMBERS
    group = 2
    rows = pl.BlockSpec((group * piece, DOUT), lambda i: (i, 0))
    out = jax.ShapeDtypeStruct((COLS, DOUT), jnp.bfloat16)
    return pl.pallas_call(
        adam_kernel,
        grid=(MEMBERS // group,),
        in_specs=[
            rows,
            pl.BlockSpec((group, piece, DOUT), lambda i: (i, 0, 0)),
            pl.BlockSpec((group, piece, DOUT), lambda i: (i, 1, 0)),
            rows,
        ],
        out_specs=[rows] * 3,
        out_shape=[out] * 3,
        compiler_params=params(),
        cost_estimate=cost(20 * COLS * DOUT, 16 * COLS * DOUT, 3 * COLS * DOUT),
        name="adam",
    )(weight, moments, moments, gradient)


def select_kernel(source_ref, x_ref, o_ref, sems):
    copies = [
        pltpu.make_async_copy(x_ref.at[source_ref[i]], o_ref.at[i], sems.at[i]) for i in range(MEMBERS)
    ]
    for copy in copies:
        copy.start()
    for copy in copies:
        copy.wait()


def select(source, pieces):
    return pl.pallas_call(
        select_kernel,
        in_specs=[pl.BlockSpec(memory_space=pltpu.SMEM), pl.BlockSpec(memory_space=pl.ANY)],
        out_specs=pl.BlockSpec(memory_space=pl.ANY),
        out_shape=jax.ShapeDtypeStruct(pieces.shape, pieces.dtype),
        scratch_shapes=[pltpu.SemaphoreType.DMA((MEMBERS,))],
        compiler_params=params(),
        cost_estimate=cost(0, 4 * pieces.size),
        name="select_pieces",
    )(source, pieces)


def swap_members(pieces):
    return lax.all_to_all(pieces, "member", split_axis=0, concat_axis=0, tiled=True)


def on_device(
    source, query_rows, key_rows, value_rows, cotangent, out_weight, first_moment, second_moment
):
    queries, keys, values = query_rows[0], key_rows[0], value_rows[0]
    half = lax.axis_index("tp") // ZED
    pieces = (MEMBERS, COLS // MEMBERS, DOUT)

    weight = swap_members(select(source, swap_members(out_weight.reshape(pieces)))).reshape(COLS, DOUT)

    own = cotangent[0]
    other = lax.ppermute(own, "tp", HALF_SWAP)
    pair = jnp.where(half == 0, jnp.stack([own, other]), jnp.stack([other, own]))
    incoming = lax.all_gather(
        pair.reshape(HALVES * CHUNK, DOUT), "tp", axis=0, tiled=True, axis_index_groups=Z_GROUPS
    )

    attended, chances = forward(queries, keys, values)
    attended = attended.reshape(TOK, COLS)

    partial = project(attended, weight)
    summed = lax.psum_scatter(
        partial, "tp", scatter_dimension=0, tiled=True, axis_index_groups=Z_GROUPS
    ).reshape(HALVES, CHUNK, DOUT)
    mine = lax.dynamic_index_in_dim(summed, half, 0, keepdims=False)
    theirs = lax.ppermute(
        lax.dynamic_index_in_dim(summed, 1 - half, 0, keepdims=False), "tp", HALF_SWAP
    )
    mixture = (mine.astype(jnp.float32) + theirs.astype(jnp.float32)).astype(jnp.bfloat16)

    gradient = gradient_of(attended, incoming)
    query_grad, key_grad, value_grad = backward(incoming, weight, queries, keys, values, chances)

    moments = jnp.concatenate([first_moment.reshape(pieces), second_moment.reshape(pieces)], axis=1)
    moments = swap_members(select(source, swap_members(moments)))
    new_weight, new_first, new_second = adam(weight, moments, gradient)
    return (
        mixture[None],
        query_grad[None],
        key_grad[None],
        value_grad[None],
        new_weight[None],
        new_first[None],
        new_second[None],
    )


def solution(mesh):
    placed = (
        P(),
        P("member", None, "tp"),
        P("member", None, "tp"),
        P("member", None, "tp"),
        P("member", "tp", None),
        P("member", "tp", None),
        P("member", "tp", None),
        P("member", "tp", None),
    )
    return jax.shard_map(
        on_device,
        mesh=mesh,
        in_specs=placed,
        out_specs=(
            P("member", "tp", None),
            P("member", None, "tp"),
            P("member", None, "tp"),
            P("member", None, "tp"),
            P("member", "tp", None),
            P("member", "tp", None),
            P("member", "tp", None),
        ),
        check_vma=False,
    )
```

time: 466 us -> 188 us (0.40); the launches traced: 458 us -> 187 us
  waiting for transfers between devices: 175 us -> 45 us
  local copies, waits for them, and re-layouts: 91.6 us -> 8.78 us
  other arithmetic: 72 us -> 3.01 us
  matrix products: 65.6 us -> 0 us
  blocking collectives: 0 us -> 57.9 us
  Pallas kernels: 0 us -> 39.1 us
  starting transfers between devices: 39.3 us -> 18.6 us
    reduce_scatter x1, waiting for transfers between devices: 137 us -> 26.5 us  [on_device(): lax.psum_scatter(partial, 'tp', scatter_dimension=0, tiled=True, axis_ind...]
    dot_general x8 -> x0, matrix products: 60.3 us -> none  [the longest x1 14.1 us: attend_back(): jnp.einsum('hqk,khd->qhd', score_grad, key_heads, preferred_element_type=...]
    all_to_all x0 -> x2, blocking collectives: none -> 57.9 us  [swap_members(): lax.all_to_all(pieces, 'member', split_axis=0, concat_axis=0, tiled=True)]
    unnamed x48 -> x32, local copies, waits for them, and re-layouts: 61.5 us -> 7 us
    all_to_all x8 -> x0, other arithmetic: 49.4 us -> none  [the longest x2 12 us: on_device(): lax.all_to_all(jnp.take(lax.all_to_all(flat_weight, 'member', split_axis=...]
    pallas_call x0 -> x7, Pallas kernels: none -> 39.1 us  [the longest x1 10.9 us: backward(): pl.pallas_call(backward_kernel, grid=(heads,), in_specs=[pl.BlockSpec((TO...]
    all_to_all x6 -> x2, waiting for transfers between devices: 37.4 us -> 10.2 us  [swap_members(): lax.all_to_all(pieces, 'member', split_axis=0, concat_axis=0, tiled=True)]
    all_to_all x6 -> x2, starting transfers between devices: 38.6 us -> 12.5 us  [swap_members(): lax.all_to_all(pieces, 'member', split_axis=0, concat_axis=0, tiled=True)]
  transfers between devices with their start and end apart: 8 -> 6, of which waited for: 6 -> 3; matrix products, arithmetic and copies ran while one was open for 44% -> 1% of each run, Pallas kernels for 0% -> 21%
where the time goes in v1:
time: 188 us; the launch traced here: 187 us
  blocking collectives  57.9 us (31%)
  waiting for transfers between devices  45 us (24%)
  Pallas kernels  39.1 us (21%)
  starting transfers between devices  18.6 us (10%)
  between operations  14.2 us (8%)
  local copies, waits for them, and re-layouts  8.78 us (5%)
  other arithmetic  3.01 us (2%)
    all_to_all x2, blocking collectives, swap_members(): lax.all_to_all(pieces, 'member', split_axis=0, concat_axis=0, tiled=True)  57.9 us
    reduce_scatter x1, waiting for transfers between devices, on_device(): lax.psum_scatter(partial, 'tp', scatter_dimension=0, tiled=True, axis_ind...  26.5 us
    all_to_all x2, starting transfers between devices, swap_members(): lax.all_to_all(pieces, 'member', split_axis=0, concat_axis=0, tiled=True)  12.5 us
    pallas_call x1, Pallas kernels, backward(): pl.pallas_call(backward_kernel, grid=(heads,), in_specs=[pl.BlockSpec((TO...  10.9 us
    all_to_all x2, waiting for transfers between devices, swap_members(): lax.all_to_all(pieces, 'member', split_axis=0, concat_axis=0, tiled=True)  10.2 us
    ppermute x1, waiting for transfers between devices, on_device(): other = lax.ppermute(own, 'tp', HALF_SWAP)  8.14 us
    pallas_call x1, Pallas kernels, adam(): pl.pallas_call(adam_kernel, grid=(MEMBERS // group,), in_specs=[rows, pl....  7.28 us
    unnamed x32, local copies, waits for them, and re-layouts  7 us
  transfers between devices with their start and end apart: 6, of which 3 were waited for; matrix products, arithmetic and copies ran while one was open for 1% of the time, Pallas kernels for 21%

profile of v1, /device:TPU:8, one launch (start us, length us, event | category | flops | bytes accessed | tf_op | source)
XLA Modules:
  0.0 186.6 jit_solution(3812139708502255749)
XLA Ops:
  7.2 0.0 copy-start.14
  7.2 0.0 copy-start.5
  7.2 0.0 all-gather.2.cloned.1.call-start
  7.2 3.1 %collective-permute-start.1 = (bf16[64,2560]{1,0:T(8,128)(2,1)}, bf16[64,2560]{1,0:T(8,128)(2,1)S(1)}, u32[]{:S(2)}, u32[]{:S(2)}) collective-permute-start(bf16[64,2560]{1,0:T(8,128)(2,1)} %bitcast.42), channel_id=1, source_target_pairs={{0,8},{1,9},{2,10},{3,11},{4,12},{5,13},{6,14},{7,15},{8,0},{9,1},... | collective-permute-start | bytes 983048 | tf_op jit(solution)/shard_map/ppermute | solution.py:284
  10.3 8.1 %collective-permute-done.1 = bf16[64,2560]{1,0:T(8,128)(2,1)S(1)} collective-permute-done((bf16[64,2560]{1,0:T(8,128)(2,1)}, bf16[64,2560]{1,0:T(8,128)(2,1)S(1)}, u32[]{:S(2)}, u32[]{:S(2)}) %collective-permute-start.1) | collective-permute-done | bytes 327712 | tf_op jit(solution)/shard_map/ppermute | solution.py:284
  18.5 2.0 %maximum_select_fusion = bf16[2,64,2560]{2,1,0:T(8,128)(2,1)} fusion(bf16[1,64,2560]{2,1,0:T(8,128)(2,1)S(1)} %bitcast.43, bf16[1,64,2560]{2,1,0:T(8,128)(2,1)} %param.12, pred[]{:T(512)S(6)} %eq.3), kind=kLoop, calls=%fused_computation.1 | loop fusion | flops 983040 | bytes 1310721 | tf_op jit(solution)/shard_map/jit(_where)/select_n | solution.py:285
  20.5 0.0 all-gather.2.cloned.1.call-update
  20.5 0.0 copy-done.14
  20.6 22.4 %all_to_all.20.x_ref = bf16[16,16,2560]{2,1,0:T(8,128)(2,1)S(1)} all-to-all(bf16[16,16,2560]{2,1,0:T(8,128)(2,1)S(1)} %bitcast.39), channel_id=1, replica_groups=mesh['member'=16,'tp'=16] {'member'}, dimensions={0} | all-to-all | bytes 2621440 | tf_op jit(solution)/shard_map/all_to_all | solution.py:271
  43.0 0.0 copy-done.5
  43.0 0.0 copy-start.6
  43.0 0.0 copy-start.8
  43.0 1.7 select_pieces.2
  44.7 6.2 %all-to-all-start.1 = ((bf16[16,16,2560]{2,1,0:T(8,128)(2,1)}), bf16[16,16,2560]{2,1,0:T(8,128)(2,1)S(1)}, u32[]{:S(2)}, u32[]{:S(2)}) async-start(bf16[16,16,2560]{2,1,0:T(8,128)(2,1)} %select_pieces.2), calls=%async_computation.1 | async-start | bytes 2621440 | tf_op jit(solution)/shard_map/all_to_all | solution.py:271
  50.9 0.0 reduce-scatter.2.cloned.1.call-start
  50.9 0.0 copy-done.6
  50.9 0.0 copy-done.8
  50.9 0.0 copy-start.10
  50.9 1.0 copy-done.10
  52.0 6.0 %attend_forward.1 = (bf16[16,64,256]{2,1,0:T(8,128)(2,1)S(1)}, bf16[2,1024,1024]{2,1,0:T(8,128)(2,1)}) custom-call(bf16[1024,256]{1,0:T(8,128)(2,1)S(1)} %bitcast.30, bf16[1024,256]{1,0:T(8,128)(2,1)S(1)} %bitcast.32, bf16[1024,256]{1,0:T(8,128)(2,1)S(1)} %bitcast.34), custom_call_target="tpu_custom_call" | custom-call | flops 1073741824 | bytes 6291456 | tf_op jit(solution)/shard_map/attend_forward/pallas_call | solution.py:79
  58.0 10.2 %all-to-all-done.1 = bf16[16,16,2560]{2,1,0:T(8,128)(2,1)S(1)} async-done(((bf16[16,16,2560]{2,1,0:T(8,128)(2,1)}), bf16[16,16,2560]{2,1,0:T(8,128)(2,1)S(1)}, u32[]{:S(2)}, u32[]{:S(2)}) %all-to-all-start.1) | async-done | bytes 1310752 | tf_op jit(solution)/shard_map/all_to_all | solution.py:271
  68.2 0.0 copy-start
  68.2 3.7 %project.1 = bf16[1024,2560]{1,0:T(8,128)(2,1)} custom-call(bf16[1024,256]{1,0:T(8,128)(2,1)S(1)} %bitcast.28, bf16[256,2560]{1,0:T(8,128)(2,1)S(1)} %bitcast.25), custom_call_target="tpu_custom_call" | custom-call | flops 1342177280 | bytes 7077888 | tf_op jit(solution)/shard_map/project/pallas_call | solution.py:103
  71.9 0.0 copy-done
  71.9 0.0 copy-start.12
  71.9 0.0 copy-start.13
  71.9 0.0 reduce-scatter.2.cloned.1.call-update
  71.9 1.3 copy-done.12
  73.2 0.4 copy-done.13
  73.6 0.2 pad_maximum_fusion
  73.8 35.5 %all_to_all.21.x_ref = bf16[16,32,2560]{2,1,0:T(8,128)(2,1)S(1)} all-to-all(bf16[16,32,2560]{2,1,0:T(8,128)(2,1)S(1)} %pad_maximum_fusion), channel_id=1, replica_groups=mesh['member'=16,'tp'=16] {'member'}, dimensions={0} | all-to-all | bytes 5242880 | tf_op jit(solution)/shard_map/all_to_all | solution.py:271
  109.3 4.1 %select_pieces.3 = bf16[16,32,2560]{2,1,0:T(8,128)(2,1)S(1)} custom-call(s32[16]{0:T(128)S(1)} %copy-done.5, bf16[16,32,2560]{2,1,0:T(8,128)(2,1)S(1)} %all_to_all.21.x_ref), custom_call_target="tpu_custom_call" | custom-call | bytes 5242880 | tf_op jit(solution)/shard_map/select_pieces/pallas_call | solution.py:258
  113.4 0.0 copy-start.3
  113.4 1.4 copy-done.3
  114.9 6.3 %all-to-all-start.3 = ((bf16[16,32,2560]{2,1,0:T(8,128)(2,1)}), bf16[16,32,2560]{2,1,0:T(8,128)(2,1)S(1)}, u32[]{:S(2)}, u32[]{:S(2)}) async-start(bf16[16,32,2560]{2,1,0:T(8,128)(2,1)} %copy-done.3), calls=%async_computation.4 | async-start | bytes 5242880 | tf_op jit(solution)/shard_map/all_to_all | solution.py:271
  121.2 0.0 all-gather.2.cloned.1.call-done.c_ref
  121.2 5.4 %weight_gradient.1.g_ref = f32[256,2560]{1,0:T(8,128)S(1)} custom-call(bf16[1024,256]{1,0:T(8,128)(2,1)S(1)} %bitcast.29, bf16[1024,2560]{1,0:T(8,128)(2,1)} %all-gather.2.cloned.1.call-done.c_ref), custom_call_target="tpu_custom_call" | custom-call | flops 1342177280 | bytes 8388608 | tf_op jit(solution)/shard_map/weight_gradient/pallas_call | solution.py:128
  126.6 0.0 copy-start.4
  126.6 1.5 copy-done.4
  128.1 26.5 %reduce-scatter.2.cloned.1.call-done = bf16[128,2560]{1,0:T(8,128)(2,1)} async-done(((bf16[1024,2560]{1,0:T(8,128)(2,1)}), bf16[128,2560]{1,0:T(8,128)(2,1)}) %reduce-scatter.2.cloned.1.call-update) | async-done | bytes 655376 | tf_op jit(solution)/shard_map/reduce_scatter | solution.py:294
  154.6 0.0 copy-start.7
  154.6 1.8 dynamic-slice_bitcast_fusion
  156.4 3.0 %collective-permute-start = (bf16[64,2560]{1,0:T(8,128)(2,1)}, bf16[64,2560]{1,0:T(8,128)(2,1)S(1)}, u32[]{:S(2)}, u32[]{:S(2)}) collective-permute-start(bf16[64,2560]{1,0:T(8,128)(2,1)} %dynamic-slice_bitcast_fusion), channel_id=1, source_target_pairs={{0,8},{1,9},{2,10},{3,11},{4,12},{5,13},{6,14},{7,15},{8,0},{9,1},... | collective-permute-start | bytes 983048 | tf_op jit(solution)/shard_map/ppermute | solution.py:298
  159.4 0.0 all-to-all-done.3.one_ref.two_ref
  159.4 0.0 copy-start.1
  159.4 1.3 copy-done.1
  160.7 0.0 copy-start.2
  160.7 0.0 copy-start.9
  160.7 0.0 copy-start.11
  160.7 7.3 %adam.1 = (bf16[256,2560]{1,0:T(8,128)(2,1)}, bf16[256,2560]{1,0:T(8,128)(2,1)}, bf16[256,2560]{1,0:T(8,128)(2,1)}) custom-call(bf16[256,2560]{1,0:T(8,128)(2,1)S(1)} %bitcast.26, bf16[16,32,2560]{2,1,0:T(8,128)(2,1)S(1)} %all-to-all-done.3.one_ref.two_ref, bf16[16,32,2560]{2,1,0:T(8,128)(2,1)S(1)} %all-to-all-done.3.one_ref.two_ref, f32[256,2560]{1,0:T(8,128)} %copy-done.4), custom_call_target="tpu_custom_call" | custom-call | flops 13107200 | bytes 10485760 | tf_op jit(solution)/shard_map/adam/pallas_call | solution.py:230
  168.0 0.0 copy-done.7
  168.0 0.0 copy-done.2
  168.0 0.0 copy-done.9
  168.0 0.0 copy-done.11
  168.0 0.0 copy-start.15
  168.0 10.9 %attend_backward.1 = (bf16[1024,256]{1,0:T(8,128)(2,1)}, bf16[1024,256]{1,0:T(8,128)(2,1)}, bf16[1024,256]{1,0:T(8,128)(2,1)}) custom-call(bf16[1024,2560]{1,0:T(8,128)(2,1)} %all-gather.2.cloned.1.call-done.c_ref, bf16[256,2560]{1,0:T(8,128)(2,1)S(1)} %bitcast.27, bf16[1024,256]{1,0:T(8,128)(2,1)S(1)} %bitcast.31, bf16[1024,256]{1,0:T(8,128)(2,1)S(1)} %bitcast.33, ...), custom_call_target="tpu_custom_call" | custom-call | flops 3489660928 | bytes 13893632 | tf_op jit(solution)/shard_map/attend_backward/pallas_call | solution.py:186
  178.9 0.0 collective-permute-done
  178.9 0.0 copy-done.15
  178.9 0.8 fusion.1
Async XLA Ops:
  7.2 13.4 %copy-start.14 = (bf16[1,256,2560]{2,1,0:T(8,128)(2,1)S(1)}, bf16[1,256,2560]{2,1,0:T(8,128)(2,1)}, u32[]{:S(2)}) copy-start(bf16[1,256,2560]{2,1,0:T(8,128)(2,1)} %param.13) | copy-start | bytes 3932164
  7.2 35.8 %copy-start.5 = (s32[16]{0:T(128)S(1)}, s32[16]{0:T(128)}, u32[]{:S(2)}) copy-start(s32[16]{0:T(128)} %source_ref.3) | copy-start | bytes 196
  7.2 114.0 %all-gather.2.cloned.1.call-start = ((), (), s32[]{:S(2)}) async-start(), calls=%async_computation.6 | async-start | bytes 5898240 | tf_op jit(solution)/shard_map/all_gather | solution.py:286
  7.2 11.3 %collective-permute-start.1 = (bf16[64,2560]{1,0:T(8,128)(2,1)}, bf16[64,2560]{1,0:T(8,128)(2,1)S(1)}, u32[]{:S(2)}, u32[]{:S(2)}) collective-permute-start(bf16[64,2560]{1,0:T(8,128)(2,1)} %bitcast.42), channel_id=1, source_target_pairs={{0,8},{1,9},{2,10},{3,11},{4,12},{5,13},{6,14},{7,15},{8,0},{9,1},... | collective-permute-start | bytes 983048 | tf_op jit(solution)/shard_map/ppermute | solution.py:284
  43.0 8.0 %copy-start.6 = (bf16[1,1024,256]{2,1,0:T(8,128)(2,1)S(1)}, bf16[1,1024,256]{2,1,0:T(8,128)(2,1)}, u32[]{:S(2)}) copy-start(bf16[1,1024,256]{2,1,0:T(8,128)(2,1)} %param.9) | copy-start | bytes 1572868
  43.0 8.0 %copy-start.8 = (bf16[1,1024,256]{2,1,0:T(8,128)(2,1)S(1)}, bf16[1,1024,256]{2,1,0:T(8,128)(2,1)}, u32[]{:S(2)}) copy-start(bf16[1,1024,256]{2,1,0:T(8,128)(2,1)} %param.10) | copy-start | bytes 1572868
  44.7 23.5 %all-to-all-start.1 = ((bf16[16,16,2560]{2,1,0:T(8,128)(2,1)}), bf16[16,16,2560]{2,1,0:T(8,128)(2,1)S(1)}, u32[]{:S(2)}, u32[]{:S(2)}) async-start(bf16[16,16,2560]{2,1,0:T(8,128)(2,1)} %select_pieces.2), calls=%async_computation.1 | async-start | bytes 2621440 | tf_op jit(solution)/shard_map/all_to_all | solution.py:271
  50.9 103.7 %reduce-scatter.2.cloned.1.call-start = ((), (), s32[]{:S(2)}) async-start(), calls=%async_computation.5 | async-start | bytes 5898240 | tf_op jit(solution)/shard_map/reduce_scatter | solution.py:294
  50.9 1.0 copy-start.10
  68.2 3.7 %copy-start = (bf16[16,16,2560]{2,1,0:T(8,128)(2,1)}, bf16[16,16,2560]{2,1,0:T(8,128)(2,1)S(1)}, u32[]{:S(2)}) copy-start(bf16[16,16,2560]{2,1,0:T(8,128)(2,1)S(1)} %all-to-all-done.1) | copy-start | bytes 3932164
  71.9 1.3 copy-start.12
  71.9 1.7 copy-start.13
  113.4 1.5 copy-start.3
  114.9 44.5 %all-to-all-start.3 = ((bf16[16,32,2560]{2,1,0:T(8,128)(2,1)}), bf16[16,32,2560]{2,1,0:T(8,128)(2,1)S(1)}, u32[]{:S(2)}, u32[]{:S(2)}) async-start(bf16[16,32,2560]{2,1,0:T(8,128)(2,1)} %copy-done.3), calls=%async_computation.4 | async-start | bytes 5242880 | tf_op jit(solution)/shard_map/all_to_all | solution.py:271
  126.6 1.5 copy-start.4
  154.6 13.4 %copy-start.7 = (bf16[1,1024,256]{2,1,0:T(8,128)(2,1)S(1)}, bf16[1,1024,256]{2,1,0:T(8,128)(2,1)}, u32[]{:S(2)}) copy-start(bf16[1,1024,256]{2,1,0:T(8,128)(2,1)} %param.9) | copy-start | bytes 1572868
  156.4 22.5 %collective-permute-start = (bf16[64,2560]{1,0:T(8,128)(2,1)}, bf16[64,2560]{1,0:T(8,128)(2,1)S(1)}, u32[]{:S(2)}, u32[]{:S(2)}) collective-permute-start(bf16[64,2560]{1,0:T(8,128)(2,1)} %dynamic-slice_bitcast_fusion), channel_id=1, source_target_pairs={{0,8},{1,9},{2,10},{3,11},{4,12},{5,13},{6,14},{7,15},{8,0},{9,1},... | collective-permute-start | bytes 983048 | tf_op jit(solution)/shard_map/ppermute | solution.py:298
  159.4 1.3 copy-start.1
  160.7 7.3 %copy-start.2 = (bf16[16,16,2560]{2,1,0:T(8,128)(2,1)S(1)}, bf16[16,16,2560]{2,1,0:T(8,128)(2,1)}, u32[]{:S(2)}) copy-start(bf16[16,16,2560]{2,1,0:T(8,128)(2,1)} %copy-done) | copy-start | bytes 3932164
  160.7 7.3 %copy-start.9 = (bf16[1,1024,256]{2,1,0:T(8,128)(2,1)S(1)}, bf16[1,1024,256]{2,1,0:T(8,128)(2,1)}, u32[]{:S(2)}) copy-start(bf16[1,1024,256]{2,1,0:T(8,128)(2,1)} %param.10) | copy-start | bytes 1572868
  160.7 7.3 %copy-start.11 = (bf16[1,1024,256]{2,1,0:T(8,128)(2,1)S(1)}, bf16[1,1024,256]{2,1,0:T(8,128)(2,1)}, u32[]{:S(2)}) copy-start(bf16[1,1024,256]{2,1,0:T(8,128)(2,1)} %param.11) | copy-start | bytes 1572868
  168.0 10.9 %copy-start.15 = (bf16[128,2560]{1,0:T(8,128)(2,1)S(1)}, bf16[128,2560]{1,0:T(8,128)(2,1)}, u32[]{:S(2)}) copy-start(bf16[128,2560]{1,0:T(8,128)(2,1)} %reduce-scatter.2.cloned.1.call-done) | copy-start | bytes 1966084
Sparse Core Ops, SparseCore 0:
  20.7 67.5 all-gather.1
  90.8 63.7 reduce-scatter.1

commit v2 on v1

--- a/solution.py
+++ b/solution.py
@@ -19,6 +19,7 @@
 VMEM_BYTES = 48 * 1024 * 1024
 
 Z_GROUPS = [[half * ZED + z for z in range(ZED)] for half in range(HALVES)]
+PAIRS = [[half * ZED + z for half in range(HALVES)] for z in range(ZED)]
 HALF_SWAP = [(t, (t + ZED) % (ZED * HALVES)) for t in range(ZED * HALVES)]
 
 NN = (((1,), (0,)), ((), ()))
@@ -216,15 +217,16 @@
     second_full = 0.999 * two_ref[...].reshape(shape).astype(jnp.float32) + 0.001 * gradient * gradient
     fix_one = 1.0 - 0.9**ADAM_STEP
     fix_two = 1.0 - 0.999**ADAM_STEP
-    update = first_full / fix_one / (jnp.sqrt(second_full / fix_two) + 1e-08)
-    nw_ref[...] = (w_ref[...].astype(jnp.float32) - 0.001 * update).astype(jnp.bfloat16)
+    spread = second_full * (1.0 / fix_two)
+    update = first_full * (0.001 / fix_one) / (spread * lax.rsqrt(spread) + 1e-08)
+    nw_ref[...] = (w_ref[...].astype(jnp.float32) - update).astype(jnp.bfloat16)
     n1_ref[...] = first_full.astype(jnp.bfloat16)
     n2_ref[...] = second_full.astype(jnp.bfloat16)
 
 
 def adam(weight, moments, gradient):
     piece = COLS // MEMBERS
-    group = 2
+    group = 8
     rows = pl.BlockSpec((group * piece, DOUT), lambda i: (i, 0))
     out = jax.ShapeDtypeStruct((COLS, DOUT), jnp.bfloat16)
     return pl.pallas_call(
@@ -280,28 +282,24 @@
 
     weight = swap_members(select(source, swap_members(out_weight.reshape(pieces)))).reshape(COLS, DOUT)
 
-    own = cotangent[0]
-    other = lax.ppermute(own, "tp", HALF_SWAP)
-    pair = jnp.where(half == 0, jnp.stack([own, other]), jnp.stack([other, own]))
-    incoming = lax.all_gather(
-        pair.reshape(HALVES * CHUNK, DOUT), "tp", axis=0, tiled=True, axis_index_groups=Z_GROUPS
-    )
+    pair = lax.all_gather(cotangent[0], "tp", axis=0, tiled=True, axis_index_groups=PAIRS)
+    incoming = lax.all_gather(pair, "tp", axis=0, tiled=True, axis_index_groups=Z_GROUPS)
 
     attended, chances = forward(queries, keys, values)
     attended = attended.reshape(TOK, COLS)
 
     partial = project(attended, weight)
+    gradient = gradient_of(attended, incoming)
+    query_grad, key_grad, value_grad = backward(incoming, weight, queries, keys, values, chances)
     summed = lax.psum_scatter(
         partial, "tp", scatter_dimension=0, tiled=True, axis_index_groups=Z_GROUPS
     ).reshape(HALVES, CHUNK, DOUT)
+    summed, query_grad, gradient = lax.optimization_barrier((summed, query_grad, gradient))
     mine = lax.dynamic_index_in_dim(summed, half, 0, keepdims=False)
     theirs = lax.ppermute(
         lax.dynamic_index_in_dim(summed, 1 - half, 0, keepdims=False), "tp", HALF_SWAP
     )
     mixture = (mine.astype(jnp.float32) + theirs.astype(jnp.float32)).astype(jnp.bfloat16)
-
-    gradient = gradient_of(attended, incoming)
-    query_grad, key_grad, value_grad = backward(incoming, weight, queries, keys, values, chances)
 
     moments = jnp.concatenate([first_moment.reshape(pieces), second_moment.reshape(pieces)], axis=1)
     moments = swap_members(select(source, swap_members(moments)))

time: 188 us -> 174 us (0.926)
  waiting for transfers between devices: 45 us -> 27.2 us
  blocking collectives: 57.9 us -> 70.6 us
  starting transfers between devices: 18.6 us -> 15.6 us
  Pallas kernels: 39.1 us -> 36.3 us
  other arithmetic: 3.01 us -> 1 us
    all_gather x0 -> x1, blocking collectives: none -> 13.4 us  [on_device(): lax.all_gather(cotangent[0], 'tp', axis=0, tiled=True, axis_index_groups=...]
    reduce_scatter x1, waiting for transfers between devices: 26.5 us -> 14.6 us  [on_device(): lax.psum_scatter(partial, 'tp', scatter_dimension=0, tiled=True, axis_ind...]
    ppermute x1 -> x0, waiting for transfers between devices: 8.14 us -> none  [on_device(): other = lax.ppermute(own, 'tp', HALF_SWAP)]
    ppermute x1 -> x0, starting transfers between devices: 3.11 us -> none  [on_device(): other = lax.ppermute(own, 'tp', HALF_SWAP)]
    pallas_call x1, Pallas kernels: 7.28 us -> 4.37 us  [adam(): pl.pallas_call(adam_kernel, grid=(MEMBERS // group,), in_specs=[rows, pl....]
    ppermute x1, waiting for transfers between devices: 0.01 us -> 2.34 us  [on_device(): lax.ppermute(lax.dynamic_index_in_dim(summed, 1 - half, 0, keepdims=False...]
    select_n x1 -> x0, other arithmetic: 2.03 us -> none  [on_device(): jnp.where(half == 0, jnp.stack([own, other]), jnp.stack([other, own]))]
    unnamed x32 -> x30, local copies, waits for them, and re-layouts: 7 us -> 7.05 us
  transfers between devices with their start and end apart: 6 -> 5, of which waited for: 3 -> 3; matrix products, arithmetic and copies ran while one was open for 1% -> 1% of each run, Pallas kernels for 21% -> 21%
where the time goes in v2:
time: 174 us; the launch traced here: 173 us
  blocking collectives  70.6 us (41%)
  Pallas kernels  36.3 us (21%)
  waiting for transfers between devices  27.2 us (16%)
  starting transfers between devices  15.6 us (9%)
  between operations  14.2 us (8%)
  local copies, waits for them, and re-layouts  8.04 us (5%)
    all_to_all x2, blocking collectives, swap_members(): lax.all_to_all(pieces, 'member', split_axis=0, concat_axis=0, tiled=True)  57.2 us
    reduce_scatter x1, waiting for transfers between devices, on_device(): lax.psum_scatter(partial, 'tp', scatter_dimension=0, tiled=True, axis_ind...  14.6 us
    all_gather x1, blocking collectives, on_device(): lax.all_gather(cotangent[0], 'tp', axis=0, tiled=True, axis_index_groups=...  13.4 us
    all_to_all x2, starting transfers between devices, swap_members(): lax.all_to_all(pieces, 'member', split_axis=0, concat_axis=0, tiled=True)  12.5 us
    pallas_call x1, Pallas kernels, backward(): pl.pallas_call(backward_kernel, grid=(heads,), in_specs=[pl.BlockSpec((TO...  10.9 us
    all_to_all x2, waiting for transfers between devices, swap_members(): lax.all_to_all(pieces, 'member', split_axis=0, concat_axis=0, tiled=True)  10.2 us
    unnamed x30, local copies, waits for them, and re-layouts  7.05 us
    pallas_call x1, Pallas kernels, forward(): pl.pallas_call(forward_kernel, grid=(heads,), in_specs=[head_block] * 3,...  6 us
  transfers between devices with their start and end apart: 5, of which 3 were waited for; matrix products, arithmetic and copies ran while one was open for 1% of the time, Pallas kernels for 21%

profile of v2, /device:TPU:8, one launch (start us, length us, event | category | flops | bytes accessed | tf_op | source)
XLA Modules:
  0.0 173.0 jit_solution(5503099563888284715)
XLA Ops:
  7.2 0.0 copy-start.5
  7.2 0.0 all-gather.4.cloned.1.call-start
  7.2 13.4 %all-gather = bf16[1,128,2560]{2,1,0:T(8,128)(2,1)} all-gather(bf16[1,64,2560]{2,1,0:T(8,128)(2,1)} %param.12), channel_id=2, replica_groups={{0,8},{1,9},{2,10},{3,11},{4,12},{5,13},{6,14},{7,15},{16,24},{17,25},{..., dimensions={1}, use_global_device_ids=true | all-gather | bytes 983040 | tf_op jit(solution)/shard_map/all_gather | solution.py:285
  20.6 0.0 all-gather.4.cloned.1.call-update
  20.6 21.7 %all_to_all.20.x_ref = bf16[16,16,2560]{2,1,0:T(8,128)(2,1)S(1)} all-to-all(bf16[16,16,2560]{2,1,0:T(8,128)(2,1)} %bitcast.38), channel_id=1, replica_groups=mesh['member'=16,'tp'=16] {'member'}, dimensions={0} | all-to-all | bytes 2621440 | tf_op jit(solution)/shard_map/all_to_all | solution.py:273
  42.3 0.0 copy-done.5
  42.3 0.0 copy-start.6
  42.3 0.0 copy-start.8
  42.3 1.7 select_pieces.2
  44.1 6.2 %all-to-all-start.1 = ((bf16[16,16,2560]{2,1,0:T(8,128)(2,1)}), bf16[16,16,2560]{2,1,0:T(8,128)(2,1)S(1)}, u32[]{:S(2)}, u32[]{:S(2)}) async-start(bf16[16,16,2560]{2,1,0:T(8,128)(2,1)} %select_pieces.2), calls=%async_computation.1 | async-start | bytes 2621440 | tf_op jit(solution)/shard_map/all_to_all | solution.py:273
  50.2 0.0 reduce-scatter.2.cloned.1.call-start
  50.3 0.0 copy-done.6
  50.3 0.0 copy-done.8
  50.3 0.0 copy-start.10
  50.3 1.0 copy-done.10
  51.4 6.0 %attend_forward.1 = (bf16[16,64,256]{2,1,0:T(8,128)(2,1)S(1)}, bf16[2,1024,1024]{2,1,0:T(8,128)(2,1)}) custom-call(bf16[1024,256]{1,0:T(8,128)(2,1)S(1)} %bitcast.28, bf16[1024,256]{1,0:T(8,128)(2,1)S(1)} %bitcast.30, bf16[1024,256]{1,0:T(8,128)(2,1)S(1)} %bitcast.32), custom_call_target="tpu_custom_call" | custom-call | flops 1073741824 | bytes 6291456 | tf_op jit(solution)/shard_map/attend_forward/pallas_call | solution.py:80
  57.4 10.2 %all-to-all-done.1 = bf16[16,16,2560]{2,1,0:T(8,128)(2,1)S(1)} async-done(((bf16[16,16,2560]{2,1,0:T(8,128)(2,1)}), bf16[16,16,2560]{2,1,0:T(8,128)(2,1)S(1)}, u32[]{:S(2)}, u32[]{:S(2)}) %all-to-all-start.1) | async-done | bytes 1310752 | tf_op jit(solution)/shard_map/all_to_all | solution.py:273
  67.6 0.0 copy-start
  67.6 3.7 %project.1 = bf16[1024,2560]{1,0:T(8,128)(2,1)} custom-call(bf16[1024,256]{1,0:T(8,128)(2,1)S(1)} %bitcast.26, bf16[256,2560]{1,0:T(8,128)(2,1)S(1)} %bitcast.23), custom_call_target="tpu_custom_call" | custom-call | flops 1342177280 | bytes 7077888 | tf_op jit(solution)/shard_map/project/pallas_call | solution.py:104
  71.3 0.0 copy-done
  71.3 0.0 copy-start.12
  71.3 0.0 copy-start.13
  71.3 0.0 reduce-scatter.2.cloned.1.call-update
  71.3 1.3 copy-done.12
  72.6 0.4 copy-done.13
  73.0 0.2 pad_maximum_fusion
  73.2 35.5 %all_to_all.21.x_ref = bf16[16,32,2560]{2,1,0:T(8,128)(2,1)S(1)} all-to-all(bf16[16,32,2560]{2,1,0:T(8,128)(2,1)S(1)} %pad_maximum_fusion), channel_id=1, replica_groups=mesh['member'=16,'tp'=16] {'member'}, dimensions={0} | all-to-all | bytes 5242880 | tf_op jit(solution)/shard_map/all_to_all | solution.py:273
  108.7 4.1 %select_pieces.3 = bf16[16,32,2560]{2,1,0:T(8,128)(2,1)S(1)} custom-call(s32[16]{0:T(128)S(1)} %copy-done.5, bf16[16,32,2560]{2,1,0:T(8,128)(2,1)S(1)} %all_to_all.21.x_ref), custom_call_target="tpu_custom_call" | custom-call | bytes 5242880 | tf_op jit(solution)/shard_map/select_pieces/pallas_call | solution.py:260
  112.8 0.0 copy-start.3
  112.9 1.4 copy-done.3
  114.3 6.3 %all-to-all-start.3 = ((bf16[16,32,2560]{2,1,0:T(8,128)(2,1)}), bf16[16,32,2560]{2,1,0:T(8,128)(2,1)S(1)}, u32[]{:S(2)}, u32[]{:S(2)}) async-start(bf16[16,32,2560]{2,1,0:T(8,128)(2,1)} %copy-done.3), calls=%async_computation.4 | async-start | bytes 5242880 | tf_op jit(solution)/shard_map/all_to_all | solution.py:273
  120.6 0.0 all-gather.4.cloned.1.call-done
  120.6 0.0 copy-start.1
  120.6 0.0 copy-start.7
  120.7 0.0 copy-start.9
  120.7 0.0 copy-start.11
  120.7 5.5 %weight_gradient.1.g_ref = f32[256,2560]{1,0:T(8,128)S(1)} custom-call(bf16[1024,256]{1,0:T(8,128)(2,1)S(1)} %bitcast.27, bf16[1024,2560]{1,0:T(8,128)(2,1)} %bitcast.34), custom_call_target="tpu_custom_call" | custom-call | flops 1342177280 | bytes 8388608 | tf_op jit(solution)/shard_map/weight_gradient/pallas_call | solution.py:129
  126.2 0.0 copy-start.4
  126.2 1.5 copy-done.4
  127.7 0.0 copy-done.1
  127.7 0.0 copy-done.7
  127.7 0.0 copy-done.9
  127.7 0.0 copy-done.11
  127.7 10.9 %attend_backward.1 = (bf16[1024,256]{1,0:T(8,128)(2,1)}, bf16[1024,256]{1,0:T(8,128)(2,1)}, bf16[1024,256]{1,0:T(8,128)(2,1)}) custom-call(bf16[1024,2560]{1,0:T(8,128)(2,1)} %bitcast.35, bf16[256,2560]{1,0:T(8,128)(2,1)S(1)} %bitcast.24, bf16[1024,256]{1,0:T(8,128)(2,1)S(1)} %bitcast.29, bf16[1024,256]{1,0:T(8,128)(2,1)S(1)} %bitcast.31, ...), custom_call_target="tpu_custom_call" | custom-call | flops 3489660928 | bytes 13893632 | tf_op jit(solution)/shard_map/attend_backward/pallas_call | solution.py:187
  138.6 14.6 %reduce-scatter.2.cloned.1.call-done = bf16[128,2560]{1,0:T(8,128)(2,1)} async-done(((bf16[1024,2560]{1,0:T(8,128)(2,1)}), bf16[128,2560]{1,0:T(8,128)(2,1)}) %reduce-scatter.2.cloned.1.call-update) | async-done | bytes 655376 | tf_op jit(solution)/shard_map/reduce_scatter | solution.py:294
  153.3 1.0 dynamic-slice_bitcast_fusion
  154.3 3.1 %collective-permute-start = (bf16[64,2560]{1,0:T(8,128)(2,1)S(1)}, bf16[64,2560]{1,0:T(8,128)(2,1)S(1)}, u32[]{:S(2)}, u32[]{:S(2)}) collective-permute-start(bf16[64,2560]{1,0:T(8,128)(2,1)S(1)} %dynamic-slice_bitcast_fusion), channel_id=1, source_target_pairs={{0,8},{1,9},{2,10},{3,11},{4,12},{5,13},{6,14},{7,15},{8,0},{9,1},... | collective-permute-start | bytes 983048 | tf_op jit(solution)/shard_map/ppermute | solution.py:299
  157.3 0.0 all-to-all-done.3.one_ref.two_ref
  157.3 0.0 copy-start.2
  157.3 1.3 copy-done.2
  158.6 0.0 copy-start.14
  158.6 4.4 %adam.1 = (bf16[256,2560]{1,0:T(8,128)(2,1)}, bf16[256,2560]{1,0:T(8,128)(2,1)}, bf16[256,2560]{1,0:T(8,128)(2,1)}) custom-call(bf16[256,2560]{1,0:T(8,128)(2,1)S(1)} %bitcast.25, bf16[16,32,2560]{2,1,0:T(8,128)(2,1)S(1)} %all-to-all-done.3.one_ref.two_ref, bf16[16,32,2560]{2,1,0:T(8,128)(2,1)S(1)} %all-to-all-done.3.one_ref.two_ref, f32[256,2560]{1,0:T(8,128)} %copy-done.4), custom_call_target="tpu_custom_call" | custom-call | flops 13107200 | bytes 10485760 | tf_op jit(solution)/shard_map/adam/pallas_call | solution.py:232
  163.0 2.3 %collective-permute-done = bf16[64,2560]{1,0:T(8,128)(2,1)S(1)} collective-permute-done((bf16[64,2560]{1,0:T(8,128)(2,1)S(1)}, bf16[64,2560]{1,0:T(8,128)(2,1)S(1)}, u32[]{:S(2)}, u32[]{:S(2)}) %collective-permute-start) | collective-permute-done | bytes 327712 | tf_op jit(solution)/shard_map/ppermute | solution.py:299
  165.4 0.0 copy-done.14
  165.4 0.8 fusion.1
Async XLA Ops:
  7.2 35.2 %copy-start.5 = (s32[16]{0:T(128)S(1)}, s32[16]{0:T(128)}, u32[]{:S(2)}) copy-start(s32[16]{0:T(128)} %source_ref.3) | copy-start | bytes 196
  7.2 113.4 %all-gather.4.cloned.1.call-start = ((), (), s32[]{:S(2)}) async-start(), calls=%async_computation.6 | async-start | bytes 5898240 | tf_op jit(solution)/shard_map/all_gather | solution.py:286
  42.3 8.0 %copy-start.6 = (bf16[1,1024,256]{2,1,0:T(8,128)(2,1)S(1)}, bf16[1,1024,256]{2,1,0:T(8,128)(2,1)}, u32[]{:S(2)}) copy-start(bf16[1,1024,256]{2,1,0:T(8,128)(2,1)} %param.9) | copy-start | bytes 1572868
  42.3 8.0 %copy-start.8 = (bf16[1,1024,256]{2,1,0:T(8,128)(2,1)S(1)}, bf16[1,1024,256]{2,1,0:T(8,128)(2,1)}, u32[]{:S(2)}) copy-start(bf16[1,1024,256]{2,1,0:T(8,128)(2,1)} %param.10) | copy-start | bytes 1572868
  44.1 23.5 %all-to-all-start.1 = ((bf16[16,16,2560]{2,1,0:T(8,128)(2,1)}), bf16[16,16,2560]{2,1,0:T(8,128)(2,1)S(1)}, u32[]{:S(2)}, u32[]{:S(2)}) async-start(bf16[16,16,2560]{2,1,0:T(8,128)(2,1)} %select_pieces.2), calls=%async_computation.1 | async-start | bytes 2621440 | tf_op jit(solution)/shard_map/all_to_all | solution.py:273
  50.2 103.0 %reduce-scatter.2.cloned.1.call-start = ((), (), s32[]{:S(2)}) async-start(), calls=%async_computation.5 | async-start | bytes 5898240 | tf_op jit(solution)/shard_map/reduce_scatter | solution.py:294
  50.3 1.1 copy-start.10
  67.6 3.7 %copy-start = (bf16[16,16,2560]{2,1,0:T(8,128)(2,1)}, bf16[16,16,2560]{2,1,0:T(8,128)(2,1)S(1)}, u32[]{:S(2)}) copy-start(bf16[16,16,2560]{2,1,0:T(8,128)(2,1)S(1)} %all-to-all-done.1) | copy-start | bytes 3932164
  71.3 1.3 copy-start.12
  71.3 1.8 %copy-start.13 = (bf16[1,256,2560]{2,1,0:T(8,128)(2,1)S(1)}, bf16[1,256,2560]{2,1,0:T(8,128)(2,1)}, u32[]{:S(2)}) copy-start(bf16[1,256,2560]{2,1,0:T(8,128)(2,1)} %param.14) | copy-start | bytes 3932164
  112.8 1.5 copy-start.3
  114.3 43.0 %all-to-all-start.3 = ((bf16[16,32,2560]{2,1,0:T(8,128)(2,1)}), bf16[16,32,2560]{2,1,0:T(8,128)(2,1)S(1)}, u32[]{:S(2)}, u32[]{:S(2)}) async-start(bf16[16,32,2560]{2,1,0:T(8,128)(2,1)} %copy-done.3), calls=%async_computation.4 | async-start | bytes 5242880 | tf_op jit(solution)/shard_map/all_to_all | solution.py:273
  120.6 7.1 %copy-start.1 = (bf16[16,16,2560]{2,1,0:T(8,128)(2,1)S(1)}, bf16[16,16,2560]{2,1,0:T(8,128)(2,1)}, u32[]{:S(2)}) copy-start(bf16[16,16,2560]{2,1,0:T(8,128)(2,1)} %copy-done) | copy-start | bytes 3932164
  120.6 7.1 %copy-start.7 = (bf16[1,1024,256]{2,1,0:T(8,128)(2,1)S(1)}, bf16[1,1024,256]{2,1,0:T(8,128)(2,1)}, u32[]{:S(2)}) copy-start(bf16[1,1024,256]{2,1,0:T(8,128)(2,1)} %param.9) | copy-start | bytes 1572868
  120.7 7.0 %copy-start.9 = (bf16[1,1024,256]{2,1,0:T(8,128)(2,1)S(1)}, bf16[1,1024,256]{2,1,0:T(8,128)(2,1)}, u32[]{:S(2)}) copy-start(bf16[1,1024,256]{2,1,0:T(8,128)(2,1)} %param.10) | copy-start | bytes 1572868
  120.7 7.0 %copy-start.11 = (bf16[1,1024,256]{2,1,0:T(8,128)(2,1)S(1)}, bf16[1,1024,256]{2,1,0:T(8,128)(2,1)}, u32[]{:S(2)}) copy-start(bf16[1,1024,256]{2,1,0:T(8,128)(2,1)} %param.11) | copy-start | bytes 1572868
  126.2 1.5 copy-start.4
  154.3 11.1 %collective-permute-start = (bf16[64,2560]{1,0:T(8,128)(2,1)S(1)}, bf16[64,2560]{1,0:T(8,128)(2,1)S(1)}, u32[]{:S(2)}, u32[]{:S(2)}) collective-permute-start(bf16[64,2560]{1,0:T(8,128)(2,1)S(1)} %dynamic-slice_bitcast_fusion), channel_id=1, source_target_pairs={{0,8},{1,9},{2,10},{3,11},{4,12},{5,13},{6,14},{7,15},{8,0},{9,1},... | collective-permute-start | bytes 983048 | tf_op jit(solution)/shard_map/ppermute | solution.py:299
  157.3 1.3 copy-start.2
  158.6 6.7 %copy-start.14 = (bf16[128,2560]{1,0:T(8,128)(2,1)S(1)}, bf16[128,2560]{1,0:T(8,128)(2,1)}, u32[]{:S(2)}) copy-start(bf16[128,2560]{1,0:T(8,128)(2,1)} %reduce-scatter.2.cloned.1.call-done) | copy-start | bytes 1966084
Sparse Core Ops, SparseCore 0:
  20.7 66.0 all-gather.3
  89.4 63.7 reduce-scatter.1

commit v3 on v2

--- a/solution.py
+++ b/solution.py
@@ -17,9 +17,10 @@
 QB = 256
 SCALE = HD ** (-0.5)
 VMEM_BYTES = 48 * 1024 * 1024
+ANYWHERE = pl.BlockSpec(memory_space=pl.ANY)
 
 Z_GROUPS = [[half * ZED + z for z in range(ZED)] for half in range(HALVES)]
-PAIRS = [[half * ZED + z for half in range(HALVES)] for z in range(ZED)]
+ORDER = [0, 7, 1, 6, 2, 5, 3, 4]
 HALF_SWAP = [(t, (t + ZED) % (ZED * HALVES)) for t in range(ZED * HALVES)]
 
 NN = (((1,), (0,)), ((), ()))
@@ -30,19 +31,26 @@
     return lax.dot_general(a, b, dims, preferred_element_type=jnp.float32)
 
 
-def params(**more):
-    return pltpu.CompilerParams(vmem_limit_bytes=VMEM_BYTES, **more)
+def params(vmem=VMEM_BYTES):
+    return pltpu.CompilerParams(vmem_limit_bytes=vmem)
 
 
 def cost(flops, nbytes, trans=0):
     return pl.CostEstimate(flops=flops, bytes_accessed=nbytes, transcendentals=trans)
 
 
-def place(t):
-    return (t % ZED) * HALVES + t // ZED
-
-
-def forward_kernel(q_ref, k_ref, v_ref, att_ref, p_ref):
+def ring(step):
+    return [(h * ZED + z, h * ZED + (z + step) % ZED) for h in range(HALVES) for z in range(ZED)]
+
+
+def token_block(z, part, spot_ref):
+    half = spot_ref[1]
+    return z + ZED * (half + part - 2 * half * part)
+
+
+def forward_kernel(spot_ref, q_ref, k_ref, v_ref, *refs):
+    att_ref, p_ref = refs[-2:]
+    half = spot_ref[1]
     keys = k_ref[...]
     values_t = v_ref[...].astype(jnp.float32).T.astype(jnp.bfloat16)
     row = lax.broadcasted_iota(jnp.int32, (QB, QB), 0)
@@ -71,16 +79,18 @@
             out_t = out_t + mm(values_t[:, :low], early, NN)
         rows = out_t.T.astype(jnp.bfloat16)
         for part in range(QB // CHUNK):
-            att_ref[place(i * (QB // CHUNK) + part)] = rows[part * CHUNK : (part + 1) * CHUNK]
-
-
-def forward(queries, keys, values):
+            t = i * (QB // CHUNK) + part
+            side = half if t < ZED else 1 - half
+            att_ref[(t % ZED) * HALVES + side] = rows[part * CHUNK : (part + 1) * CHUNK]
+
+
+def forward(spot, queries, keys, values, after):
     heads = COLS // HD
     head_block = pl.BlockSpec((TOK, HD), lambda h: (0, h))
     return pl.pallas_call(
         forward_kernel,
         grid=(heads,),
-        in_specs=[head_block] * 3,
+        in_specs=[pl.BlockSpec(memory_space=pltpu.SMEM)] + [head_block] * 3 + [ANYWHERE] * len(after),
         out_specs=[
             pl.BlockSpec((ZED * HALVES, CHUNK, HD), lambda h: (0, 0, h)),
             pl.BlockSpec((1, TOK, TOK), lambda h: (h, 0, 0)),
@@ -92,14 +102,15 @@
         compiler_params=params(),
         cost_estimate=cost(4 * TOK * TOK * COLS, 8 * TOK * COLS + 2 * heads * TOK * TOK, heads * TOK * TOK),
         name="attend_forward",
-    )(queries, keys, values)
-
-
-def project_kernel(a_ref, w_ref, o_ref):
+    )(spot, queries, keys, values, *after)
+
+
+def project_kernel(a_ref, w_ref, *refs):
+    o_ref = refs[-1]
     o_ref[...] = mm(a_ref[...], w_ref[...], NN).astype(jnp.bfloat16)
 
 
-def project(attended, weight):
+def project(attended, weight, after):
     block = 256
     return pl.pallas_call(
         project_kernel,
@@ -107,54 +118,81 @@
         in_specs=[
             pl.BlockSpec((block, COLS), lambda i: (i, 0)),
             pl.BlockSpec((COLS, DOUT), lambda i: (0, 0)),
-        ],
+        ]
+        + [ANYWHERE] * len(after),
         out_specs=pl.BlockSpec((block, DOUT), lambda i: (i, 0)),
         out_shape=jax.ShapeDtypeStruct((TOK, DOUT), jnp.bfloat16),
         compiler_params=params(),
         cost_estimate=cost(2 * TOK * COLS * DOUT, 2 * (TOK * COLS + COLS * DOUT + TOK * DOUT)),
         name="project",
-    )(attended, weight)
-
-
-def gradient_kernel(a_ref, c_ref, o_ref, t_ref):
+    )(attended, weight, *after)
+
+
+def rows_at(place, own_ref, cot_refs, spot_ref):
+    z = lax.rem(spot_ref[0] + ORDER[place], ZED)
+    return [own_ref[z], cot_refs[place][...]]
+
+
+def gradient_kernel(spot_ref, a_ref, own_ref, *refs):
+    cot_refs, (o_ref, t_ref) = refs[: len(ORDER)], refs[len(ORDER) :]
+
     @pl.when(pl.program_id(0) == 0)
     def _():
-        t_ref[...] = a_ref[...].astype(jnp.float32).T.astype(jnp.bfloat16)
-
-    o_ref[...] = mm(t_ref[...], c_ref[...], NN)
-
-
-def gradient_of(attended, incoming):
+        for place, offset in enumerate(ORDER):
+            z = lax.rem(spot_ref[0] + offset, ZED)
+            rows = a_ref[pl.ds(z * HALVES, HALVES)].reshape(HALVES * CHUNK, COLS)
+            t_ref[:, place * HALVES * CHUNK : (place + 1) * HALVES * CHUNK] = (
+                rows.astype(jnp.float32).T.astype(jnp.bfloat16)
+            )
+
+    total = None
+    width = 2 * HALVES * CHUNK
+    for pair in range(len(ORDER) // 2):
+        rows = jnp.concatenate(
+            [r for place in (2 * pair, 2 * pair + 1) for r in rows_at(place, own_ref, cot_refs, spot_ref)], axis=0
+        )
+        term = mm(t_ref[:, pair * width : (pair + 1) * width], rows, NN)
+        total = term if total is None else total + term
+    o_ref[...] = total
+
+
+def gradient_of(spot, attended, gathered, incoming):
     block = 512
     return pl.pallas_call(
         gradient_kernel,
         grid=(DOUT // block,),
         in_specs=[
-            pl.BlockSpec((TOK, COLS), lambda i: (0, 0)),
-            pl.BlockSpec((TOK, block), lambda i: (0, i)),
-        ],
+            pl.BlockSpec(memory_space=pltpu.SMEM),
+            pl.BlockSpec((ZED * HALVES, CHUNK, COLS), lambda i: (0, 0, 0)),
+            pl.BlockSpec((ZED, CHUNK, block), lambda i: (0, 0, i)),
+        ]
+        + [pl.BlockSpec((CHUNK, block), lambda i: (0, i))] * len(ORDER),
         out_specs=pl.BlockSpec((COLS, block), lambda i: (0, i)),
         out_shape=jax.ShapeDtypeStruct((COLS, DOUT), jnp.float32),
         scratch_shapes=[pltpu.VMEM((COLS, TOK), jnp.bfloat16)],
-        compiler_params=params(),
+        compiler_params=params(59400000),
         cost_estimate=cost(2 * TOK * COLS * DOUT, 2 * TOK * (COLS + DOUT) + 4 * COLS * DOUT),
         name="weight_gradient",
-    )(attended, incoming)
-
-
-def backward_kernel(c_ref, w_ref, q_ref, k_ref, v_ref, p_ref, dq_ref, dk_ref, dv_ref, u_ref, ak_ref, av_ref):
+    )(spot, attended, gathered, *incoming)
+
+
+def backward_kernel(spot_ref, own_ref, *refs):
+    cot_refs, refs = refs[: len(ORDER)], refs[len(ORDER) :]
+    w_ref, q_ref, k_ref, v_ref, p_ref, dq_ref, dk_ref, dv_ref, u_ref, ak_ref, av_ref = refs
     head = pl.program_id(0)
 
     @pl.when(head == 0)
     def _():
-        step = 256
-        for block in range(TOK // step):
-            rows = mm(c_ref[block * step : (block + 1) * step, :], w_ref[...], NT).astype(jnp.bfloat16)
-            for part in range(step // CHUNK):
-                spot = block * (step // CHUNK) + part
-                t = (spot % HALVES) * ZED + spot // HALVES
+        for place in range(0, len(ORDER), 2):
+            rows = jnp.concatenate(
+                [r for p in (place, place + 1) for r in rows_at(p, own_ref, cot_refs, spot_ref)], axis=0
+            )
+            rows = mm(rows, w_ref[...], NT).astype(jnp.bfloat16)
+            for part in range(2 * HALVES):
+                z = lax.rem(spot_ref[0] + ORDER[place + part // HALVES], ZED)
+                t = token_block(z, part % HALVES, spot_ref)
                 for h in range(COLS // HD):
-                    u_ref[h, t * CHUNK : (t + 1) * CHUNK, :] = rows[
+                    u_ref[h, pl.ds(t * CHUNK, CHUNK), :] = rows[
                         part * CHUNK : (part + 1) * CHUNK, h * HD : (h + 1) * HD
                     ]
 
@@ -181,14 +219,18 @@
     dk_ref[...] = ak_ref[...].astype(jnp.bfloat16)
 
 
-def backward(incoming, weight, queries, keys, values, chances):
+def backward(spot, gathered, incoming, weight, queries, keys, values, chances):
     heads = COLS // HD
     head_block = pl.BlockSpec((TOK, HD), lambda h: (0, h))
     return pl.pallas_call(
         backward_kernel,
         grid=(heads,),
         in_specs=[
-            pl.BlockSpec((TOK, DOUT), lambda h: (0, 0)),
+            pl.BlockSpec(memory_space=pltpu.SMEM),
+            pl.BlockSpec((ZED, CHUNK, DOUT), lambda h: (0, 0, 0)),
+        ]
+        + [pl.BlockSpec((CHUNK, DOUT), lambda h: (0, 0))] * len(ORDER)
+        + [
             pl.BlockSpec((COLS, DOUT), lambda h: (0, 0)),
             head_block,
             head_block,
@@ -202,12 +244,12 @@
             pltpu.VMEM((TOK, HD), jnp.float32),
             pltpu.VMEM((TOK, HD), jnp.float32),
         ],
-        compiler_params=params(),
+        compiler_params=params(59400000),
         cost_estimate=cost(
             2 * TOK * COLS * DOUT + 8 * TOK * TOK * COLS, 2 * (TOK * DOUT + COLS * DOUT + 6 * TOK * COLS + heads * TOK * TOK)
         ),
         name="attend_backward",
-    )(incoming, weight, queries, keys, values, chances)
+    )(spot, gathered, *incoming, weight, queries, keys, values, chances)
 
 
 def adam_kernel(w_ref, one_ref, two_ref, g_ref, nw_ref, n1_ref, n2_ref):
@@ -240,13 +282,14 @@
         ],
         out_specs=[rows] * 3,
         out_shape=[out] * 3,
-        compiler_params=params(),
+        compiler_params=params(59400000),
         cost_estimate=cost(20 * COLS * DOUT, 16 * COLS * DOUT, 3 * COLS * DOUT),
         name="adam",
     )(weight, moments, moments, gradient)
 
 
-def select_kernel(source_ref, x_ref, o_ref, sems):
+def select_kernel(source_ref, x_ref, *refs):
+    o_ref, sems = refs[-2:]
     copies = [
         pltpu.make_async_copy(x_ref.at[source_ref[i]], o_ref.at[i], sems.at[i]) for i in range(MEMBERS)
     ]
@@ -256,17 +299,18 @@
         copy.wait()
 
 
-def select(source, pieces):
+def select(source, pieces, after, weighed):
     return pl.pallas_call(
         select_kernel,
-        in_specs=[pl.BlockSpec(memory_space=pltpu.SMEM), pl.BlockSpec(memory_space=pl.ANY)],
-        out_specs=pl.BlockSpec(memory_space=pl.ANY),
+        in_specs=[pl.BlockSpec(memory_space=pltpu.SMEM), pl.BlockSpec(memory_space=pltpu.VMEM)]
+        + [ANYWHERE] * len(after),
+        out_specs=ANYWHERE,
         out_shape=jax.ShapeDtypeStruct(pieces.shape, pieces.dtype),
         scratch_shapes=[pltpu.SemaphoreType.DMA((MEMBERS,))],
         compiler_params=params(),
-        cost_estimate=cost(0, 4 * pieces.size),
+        cost_estimate=cost(0, weighed * pieces.size),
         name="select_pieces",
-    )(source, pieces)
+    )(source, pieces, *after)
 
 
 def swap_members(pieces):
@@ -277,32 +321,40 @@
     source, query_rows, key_rows, value_rows, cotangent, out_weight, first_moment, second_moment
 ):
     queries, keys, values = query_rows[0], key_rows[0], value_rows[0]
-    half = lax.axis_index("tp") // ZED
     pieces = (MEMBERS, COLS // MEMBERS, DOUT)
 
-    weight = swap_members(select(source, swap_members(out_weight.reshape(pieces)))).reshape(COLS, DOUT)
-
-    pair = lax.all_gather(cotangent[0], "tp", axis=0, tiled=True, axis_index_groups=PAIRS)
-    incoming = lax.all_gather(pair, "tp", axis=0, tiled=True, axis_index_groups=Z_GROUPS)
-
-    attended, chances = forward(queries, keys, values)
-    attended = attended.reshape(TOK, COLS)
-
-    partial = project(attended, weight)
-    gradient = gradient_of(attended, incoming)
-    query_grad, key_grad, value_grad = backward(incoming, weight, queries, keys, values, chances)
+    place = lax.axis_index("tp")
+    spot = jnp.stack([place % ZED, place // ZED]).astype(jnp.int32)
+    own = cotangent[0]
+    gathered = lax.all_gather(own, "tp", axis=0, axis_index_groups=Z_GROUPS)
+    moments = jnp.concatenate([first_moment.reshape(pieces), second_moment.reshape(pieces)], axis=1)
+    attended, chances = forward(spot, queries, keys, values, [])
+
+    other = lax.ppermute(own, "tp", HALF_SWAP)
+    weight = swap_members(select(source, swap_members(out_weight.reshape(pieces)), [other, attended, moments], 4)).reshape(COLS, DOUT)
+    up, down, incoming = other, other, [other]
+    for _ in range(ZED // 2 - 1):
+        up = lax.ppermute(up, "tp", ring(1))
+        down = lax.ppermute(down, "tp", ring(-1))
+        incoming += [up, down]
+    split = CHUNK // 2
+    across = [lax.ppermute(up[:split], "tp", ring(1)), lax.ppermute(down[split:], "tp", ring(-1))]
+    incoming.append(jnp.concatenate(across, axis=0))
+
+    partial = project(attended.reshape(TOK, COLS), weight, incoming[3:5])
+    moments = swap_members(select(source, swap_members(moments), incoming[5:], 4))
+    gradient = gradient_of(spot, attended, gathered, incoming)
+    query_grad, key_grad, value_grad = backward(
+        spot, gathered, incoming, weight, queries, keys, values, chances
+    )
+
     summed = lax.psum_scatter(
         partial, "tp", scatter_dimension=0, tiled=True, axis_index_groups=Z_GROUPS
-    ).reshape(HALVES, CHUNK, DOUT)
+    )
     summed, query_grad, gradient = lax.optimization_barrier((summed, query_grad, gradient))
-    mine = lax.dynamic_index_in_dim(summed, half, 0, keepdims=False)
-    theirs = lax.ppermute(
-        lax.dynamic_index_in_dim(summed, 1 - half, 0, keepdims=False), "tp", HALF_SWAP
-    )
-    mixture = (mine.astype(jnp.float32) + theirs.astype(jnp.float32)).astype(jnp.bfloat16)
-
-    moments = jnp.concatenate([first_moment.reshape(pieces), second_moment.reshape(pieces)], axis=1)
-    moments = swap_members(select(source, swap_members(moments)))
+    theirs = lax.ppermute(summed[CHUNK:], "tp", HALF_SWAP)
+    mixture = (summed[:CHUNK].astype(jnp.float32) + theirs.astype(jnp.float32)).astype(jnp.bfloat16)
+
     new_weight, new_first, new_second = adam(weight, moments, gradient)
     return (
         mixture[None],

time: 174 us -> 172 us (0.989)
  blocking collectives: 70.6 us -> 0 us
  waiting for transfers between devices: 27.2 us -> 64.6 us
  starting transfers between devices: 15.6 us -> 43.7 us
  local copies, waits for them, and re-layouts: 8.04 us -> 4.35 us
  Pallas kernels: 36.3 us -> 38.9 us
  other arithmetic: 1 us -> 3.5 us
    all_to_all x2 -> x0, blocking collectives: 57.2 us -> none  [swap_members(): lax.all_to_all(pieces, 'member', split_axis=0, concat_axis=0, tiled=True)]
    ppermute x1 -> x10, waiting for transfers between devices: 2.34 us -> 50.2 us  [the longest x3 27.7 us: on_device(): up = lax.ppermute(up, 'tp', ring(1))]
    ppermute x1 -> x10, starting transfers between devices: 3.07 us -> 21.4 us  [the longest x3 10.5 us: on_device(): down = lax.ppermute(down, 'tp', ring(-1))]
    all_gather x1 -> x0, blocking collectives: 13.4 us -> none  [on_device(): lax.all_gather(cotangent[0], 'tp', axis=0, tiled=True, axis_index_groups=...]
    all_to_all x2 -> x4, starting transfers between devices: 12.5 us -> 22.2 us  [swap_members(): lax.all_to_all(pieces, 'member', split_axis=0, concat_axis=0, tiled=True)]
    reduce_scatter x1, waiting for transfers between devices: 14.6 us -> 5.55 us  [on_device(): lax.psum_scatter(partial, 'tp', scatter_dimension=0, tiled=True, axis_ind...]
    unnamed x30 -> x41, local copies, waits for them, and re-layouts: 7.05 us -> 2.6 us
    all_to_all x2 -> x4, waiting for transfers between devices: 10.2 us -> 8.08 us  [swap_members(): lax.all_to_all(pieces, 'member', split_axis=0, concat_axis=0, tiled=True)]
  transfers between devices with their start and end apart: 5 -> 16, of which waited for: 3 -> 10; matrix products, arithmetic and copies ran while one was open for 1% -> 2% of each run, Pallas kernels for 21% -> 23%
where the time goes in v3:
time: 172 us; the launch traced here: 169 us
  waiting for transfers between devices  64.6 us (38%)
  starting transfers between devices  43.7 us (25%)
  Pallas kernels  38.9 us (23%)
  between operations  14.2 us (8%)
  local copies, waits for them, and re-layouts  4.35 us (3%)
  other arithmetic  3.5 us (2%)
    ppermute x3, waiting for transfers between devices, on_device(): up = lax.ppermute(up, 'tp', ring(1))  27.7 us
    all_to_all x4, starting transfers between devices, swap_members(): lax.all_to_all(pieces, 'member', split_axis=0, concat_axis=0, tiled=True)  22.2 us
    ppermute x1, waiting for transfers between devices, on_device(): other = lax.ppermute(own, 'tp', HALF_SWAP)  12.9 us
    pallas_call x1, Pallas kernels, backward(): pl.pallas_call(backward_kernel, grid=(heads,), in_specs=[pl.BlockSpec(mem...  11.6 us
    ppermute x3, starting transfers between devices, on_device(): down = lax.ppermute(down, 'tp', ring(-1))  10.5 us
    all_to_all x4, waiting for transfers between devices, swap_members(): lax.all_to_all(pieces, 'member', split_axis=0, concat_axis=0, tiled=True)  8.08 us
    pallas_call x1, Pallas kernels, gradient_of(): pl.pallas_call(gradient_kernel, grid=(DOUT // block,), in_specs=[pl.Block...  7.03 us
    pallas_call x1, Pallas kernels, forward(): pl.pallas_call(forward_kernel, grid=(heads,), in_specs=[pl.BlockSpec(memo...  6.52 us
  transfers between devices with their start and end apart: 16, of which 10 were waited for; matrix products, arithmetic and copies ran while one was open for 2% of the time, Pallas kernels for 23%

profile of v3, /device:TPU:8, one launch (start us, length us, event | category | flops | bytes accessed | tf_op | source)
XLA Modules:
  0.0 169.3 jit_solution(3086640808314921495)
XLA Ops:
  7.2 0.0 copy-start.19
  7.2 0.0 copy-start.10
  7.2 0.0 copy-start.11
  7.2 0.0 all-gather.2.cloned.1.call-start
  7.2 0.7 all-gather.2.cloned.1.call-update
  7.9 5.9 %all-to-all-start = ((bf16[16,16,2560]{2,1,0:T(8,128)(2,1)}), bf16[16,16,2560]{2,1,0:T(8,128)(2,1)S(1)}, u32[]{:S(2)}, u32[]{:S(2)}) async-start(bf16[16,16,2560]{2,1,0:T(8,128)(2,1)} %bitcast.31), calls=%async_computation | async-start | bytes 2621440 | tf_op jit(solution)/shard_map/all_to_all | solution.py:317
  13.8 0.0 copy-done.19
  13.8 2.8 %collective-permute-start = (bf16[64,2560]{1,0:T(8,128)(2,1)S(1)}, bf16[64,2560]{1,0:T(8,128)(2,1)S(1)}, u32[]{:S(2)}, u32[]{:S(2)}) collective-permute-start(bf16[64,2560]{1,0:T(8,128)(2,1)S(1)} %bitcast.32), channel_id=1, source_target_pairs={{0,8},{1,9},{2,10},{3,11},{4,12},{5,13},{6,14},{7,15},{8,0},{9,1},... | collective-permute-start | bytes 983048 | tf_op jit(solution)/shard_map/ppermute | solution.py:333
  16.6 0.1 pad_add_fusion.spot_ref
  16.7 0.0 copy-done.10
  16.7 0.0 copy-done.11
  16.7 1.0 copy-done.12
  17.8 6.5 %attend_forward.1 = (bf16[16,64,256]{2,1,0:T(8,128)(2,1)S(1)}, bf16[2,1024,1024]{2,1,0:T(8,128)(2,1)}) custom-call(s32[2]{0:T(128)S(1)} %pad_add_fusion.spot_ref, bf16[1024,256]{1,0:T(8,128)(2,1)S(1)} %bitcast.24, bf16[1024,256]{1,0:T(8,128)(2,1)S(1)} %bitcast.26, bf16[1024,256]{1,0:T(8,128)(2,1)S(1)} %bitcast.28), custom_call_target="tpu_custom_call" | custom-call | flops 1073741824 | bytes 6291456 | tf_op jit(solution)/shard_map/attend_forward/pallas_call | solution.py:90
  24.3 0.0 copy-done.14
  24.3 0.0 copy-done.15
  24.3 0.0 copy-start.8
  24.3 1.6 pad_maximum_fusion.refs_2_
  26.0 0.0 copy-done.9
  26.0 12.9 %collective-permute-done.refs_0_ = bf16[64,2560]{1,0:T(8,128)(2,1)S(1)} collective-permute-done((bf16[64,2560]{1,0:T(8,128)(2,1)S(1)}, bf16[64,2560]{1,0:T(8,128)(2,1)S(1)}, u32[]{:S(2)}, u32[]{:S(2)}) %collective-permute-start) | collective-permute-done | bytes 327712 | tf_op jit(solution)/shard_map/ppermute | solution.py:333
  38.9 0.0 all-to-all-done.x_ref
  38.9 0.0 copy-done.8
  38.9 1.8 %select_pieces.2 = bf16[16,16,2560]{2,1,0:T(8,128)(2,1)} custom-call(s32[16]{0:T(128)S(1)} %copy-done.8, bf16[16,16,2560]{2,1,0:T(8,128)(2,1)S(1)} %all-to-all-done.x_ref, bf16[64,2560]{1,0:T(8,128)(2,1)S(1)} %collective-permute-done.refs_0_, bf16[16,64,256]{2,1,0:T(8,128)(2,1)S(1)} %get-tuple-element.18.refs_1_.a_ref, ...), custom_call_target="tpu_custom_call" | custom-call | bytes 2621440 | tf_op jit(solution)/shard_map/select_pieces/pallas_call | solution.py:303
  40.7 5.5 %all-to-all-start.1 = ((bf16[16,16,2560]{2,1,0:T(8,128)(2,1)}), bf16[16,16,2560]{2,1,0:T(8,128)(2,1)S(1)}, u32[]{:S(2)}, u32[]{:S(2)}) async-start(bf16[16,16,2560]{2,1,0:T(8,128)(2,1)} %select_pieces.2), calls=%async_computation.1 | async-start | bytes 2621440 | tf_op jit(solution)/shard_map/all_to_all | solution.py:317
  46.2 0.0 reduce-scatter.2.cloned.1.call-start
  46.2 2.0 %collective-permute-start.1 = (bf16[64,2560]{1,0:T(8,128)(2,1)S(1)}, bf16[64,2560]{1,0:T(8,128)(2,1)S(1)}, u32[]{:S(2)}, u32[]{:S(2)}) collective-permute-start(bf16[64,2560]{1,0:T(8,128)(2,1)S(1)} %collective-permute-done.refs_0_), channel_id=1, source_target_pairs={{0,1},{1,2},{2,3},{3,4},{4,5},{5,6},{6,7},{7,0},{8,9},{9,10},{10,1... | collective-permute-start | bytes 983048 | tf_op jit(solution)/shard_map/ppermute | solution.py:337
  48.2 0.0 copy-done.5
  48.2 4.0 %collective-permute-start.3 = (bf16[64,2560]{1,0:T(8,128)(2,1)S(1)}, bf16[64,2560]{1,0:T(8,128)(2,1)S(1)}, u32[]{:S(2)}, u32[]{:S(2)}) collective-permute-start(bf16[64,2560]{1,0:T(8,128)(2,1)S(1)} %collective-permute-done.refs_0_), channel_id=1, source_target_pairs={{0,7},{1,0},{2,1},{3,2},{4,3},{5,4},{6,5},{7,6},{8,15},{9,8},{10,9... | collective-permute-start | bytes 983048 | tf_op jit(solution)/shard_map/ppermute | solution.py:338
  52.3 8.7 %collective-permute-done.1.refs_1_ = bf16[64,2560]{1,0:T(8,128)(2,1)S(1)} collective-permute-done((bf16[64,2560]{1,0:T(8,128)(2,1)S(1)}, bf16[64,2560]{1,0:T(8,128)(2,1)S(1)}, u32[]{:S(2)}, u32[]{:S(2)}) %collective-permute-start.1) | collective-permute-done | bytes 327712 | tf_op jit(solution)/shard_map/ppermute | solution.py:337
  61.0 0.0 collective-permute-start.2
  61.0 0.0 collective-permute-done.3.refs_2_
  61.0 0.0 copy-start.18
  61.0 3.2 %collective-permute-start.4 = (bf16[64,2560]{1,0:T(8,128)(2,1)S(1)}, bf16[64,2560]{1,0:T(8,128)(2,1)S(1)}, u32[]{:S(2)}, u32[]{:S(2)}) collective-permute-start(bf16[64,2560]{1,0:T(8,128)(2,1)S(1)} %collective-permute-done.3.refs_2_), channel_id=1, source_target_pairs={{0,7},{1,0},{2,1},{3,2},{4,3},{5,4},{6,5},{7,6},{8,15},{9,8},{10,9... | collective-permute-start | bytes 983048 | tf_op jit(solution)/shard_map/ppermute | solution.py:338
  64.2 7.5 %collective-permute-done.2.refs_0_.refs_3_ = bf16[64,2560]{1,0:T(8,128)(2,1)S(1)} collective-permute-done((bf16[64,2560]{1,0:T(8,128)(2,1)S(1)}, bf16[64,2560]{1,0:T(8,128)(2,1)S(1)}, u32[]{:S(2)}, u32[]{:S(2)}) %collective-permute-start.2) | collective-permute-done | bytes 327712 | tf_op jit(solution)/shard_map/ppermute | solution.py:337
  71.8 0.0 collective-permute-done.4.refs_1_.refs_4_
  71.8 0.0 all-to-all-done.1
  71.8 0.0 copy-start
  71.8 3.8 %project.1 = bf16[1024,2560]{1,0:T(8,128)(2,1)} custom-call(bf16[1024,256]{1,0:T(8,128)(2,1)S(1)} %bitcast.22, bf16[256,2560]{1,0:T(8,128)(2,1)S(1)} %bitcast.19, bf16[64,2560]{1,0:T(8,128)(2,1)S(1)} %collective-permute-done.2.refs_0_.refs_3_, bf16[64,2560]{1,0:T(8,128)(2,1)S(1)} %collective-permute-done.4.refs_1_.refs_4_), custom_call_target="tpu_custom_call" | custom-call | flops 1342177280 | bytes 7077888 | tf_op jit(solution)/shard_map/project/pallas_call | solution.py:115
  75.6 0.0 reduce-scatter.2.cloned.1.call-update
  75.6 5.6 %all-to-all-start.2 = ((bf16[16,32,2560]{2,1,0:T(8,128)(2,1)}), bf16[16,32,2560]{2,1,0:T(8,128)(2,1)}, u32[]{:S(2)}, u32[]{:S(2)}) async-start(bf16[16,32,2560]{2,1,0:T(8,128)(2,1)} %pad_maximum_fusion.refs_2_), calls=%async_computation.3 | async-start | bytes 5242880 | tf_op jit(solution)/shard_map/all_to_all | solution.py:317
  81.2 0.0 copy-done.6
  81.2 0.1 collective-permute-start.5
  81.3 0.0 copy-done.7
  81.3 3.2 %collective-permute-start.6 = (bf16[64,2560]{1,0:T(8,128)(2,1)S(1)}, bf16[64,2560]{1,0:T(8,128)(2,1)S(1)}, u32[]{:S(2)}, u32[]{:S(2)}) collective-permute-start(bf16[64,2560]{1,0:T(8,128)(2,1)S(1)} %collective-permute-done.4.refs_1_.refs_4_), channel_id=1, source_target_pairs={{0,7},{1,0},{2,1},{3,2},{4,3},{5,4},{6,5},{7,6},{8,15},{9,8},{10,9... | collective-permute-start | bytes 983048 | tf_op jit(solution)/shard_map/ppermute | solution.py:338
  84.6 11.4 %collective-permute-done.5.refs_5_.refs_0_ = bf16[64,2560]{1,0:T(8,128)(2,1)S(1)} collective-permute-done((bf16[64,2560]{1,0:T(8,128)(2,1)S(1)}, bf16[64,2560]{1,0:T(8,128)(2,1)S(1)}, u32[]{:S(2)}, u32[]{:S(2)}) %collective-permute-start.5) | collective-permute-done | bytes 327712 | tf_op jit(solution)/shard_map/ppermute | solution.py:337
  96.0 0.1 collective-permute-start.7
  96.1 2.6 %collective-permute-done.6.refs_6_.refs_1_ = bf16[64,2560]{1,0:T(8,128)(2,1)S(1)} collective-permute-done((bf16[64,2560]{1,0:T(8,128)(2,1)S(1)}, bf16[64,2560]{1,0:T(8,128)(2,1)S(1)}, u32[]{:S(2)}, u32[]{:S(2)}) %collective-permute-start.6) | collective-permute-done | bytes 327712 | tf_op jit(solution)/shard_map/ppermute | solution.py:338
  98.6 3.8 %collective-permute-start.8 = (bf16[32,2560]{1,0:T(8,128)(2,1)S(1)}, bf16[32,2560]{1,0:T(8,128)(2,1)S(1)}, u32[]{:S(2)}, u32[]{:S(2)}) collective-permute-start(bf16[32,2560]{1,0:T(8,128)(2,1)S(1)} %slice.17), channel_id=1, source_target_pairs={{0,7},{1,0},{2,1},{3,2},{4,3},{5,4},{6,5},{7,6},{8,15},{9,8},{10,9... | collective-permute-start | bytes 491528 | tf_op jit(solution)/shard_map/ppermute | solution.py:341
  102.4 4.5 %collective-permute-done.7 = bf16[32,2560]{1,0:T(8,128)(2,1)S(1)} collective-permute-done((bf16[32,2560]{1,0:T(8,128)(2,1)S(1)}, bf16[32,2560]{1,0:T(8,128)(2,1)S(1)}, u32[]{:S(2)}, u32[]{:S(2)}) %collective-permute-start.7) | collective-permute-done | bytes 163872 | tf_op jit(solution)/shard_map/ppermute | solution.py:341
  106.9 2.6 %collective-permute-done.8 = bf16[32,2560]{1,0:T(8,128)(2,1)S(1)} collective-permute-done((bf16[32,2560]{1,0:T(8,128)(2,1)S(1)}, bf16[32,2560]{1,0:T(8,128)(2,1)S(1)}, u32[]{:S(2)}, u32[]{:S(2)}) %collective-permute-start.8) | collective-permute-done | bytes 163872 | tf_op jit(solution)/shard_map/ppermute | solution.py:341
  109.5 0.0 copy-start.4
  109.5 3.8 %all-to-all-done.2.x_ref = bf16[16,32,2560]{2,1,0:T(8,128)(2,1)} async-done(((bf16[16,32,2560]{2,1,0:T(8,128)(2,1)}), bf16[16,32,2560]{2,1,0:T(8,128)(2,1)}, u32[]{:S(2)}, u32[]{:S(2)}) %all-to-all-start.2) | async-done | bytes 2621472 | tf_op jit(solution)/shard_map/all_to_all | solution.py:317
  113.3 3.4 %select_pieces.3 = bf16[16,32,2560]{2,1,0:T(8,128)(2,1)} custom-call(s32[16]{0:T(128)S(1)} %copy-done.8, bf16[16,32,2560]{2,1,0:T(8,128)(2,1)} %all-to-all-done.2.x_ref, bf16[64,2560]{1,0:T(8,128)(2,1)S(1)} %collective-permute-done.5.refs_5_.refs_0_, bf16[64,2560]{1,0:T(8,128)(2,1)S(1)} %collective-permute-done.6.refs_6_.refs_1_, ...), custom_call_target="tpu_custom_call" | custom-call | bytes 5242880 | tf_op jit(solution)/shard_map/select_pieces/pallas_call | solution.py:303
  116.7 5.3 %all-to-all-start.3 = ((bf16[16,32,2560]{2,1,0:T(8,128)(2,1)}), bf16[16,32,2560]{2,1,0:T(8,128)(2,1)S(1)}, u32[]{:S(2)}, u32[]{:S(2)}) async-start(bf16[16,32,2560]{2,1,0:T(8,128)(2,1)} %select_pieces.3), calls=%async_computation.4 | async-start | bytes 5242880 | tf_op jit(solution)/shard_map/all_to_all | solution.py:317
  122.0 0.0 all-gather.2.cloned.1.call-done.own_ref
  122.0 7.0 %weight_gradient.1.g_ref = f32[256,2560]{1,0:T(8,128)} custom-call(s32[2]{0:T(128)} %copy-done.9, bf16[16,64,256]{2,1,0:T(8,128)(2,1)} %copy-done.1, bf16[8,64,2560]{2,1,0:T(8,128)(2,1)} %all-gather.2.cloned.1.call-done.own_ref, bf16[64,2560]{1,0:T(8,128)(2,1)} %copy-done.5, bf16[64,2560]{1,0:T(8,128)(2,1)} %copy-done.17, bf16[64,2560]{1,0:T(8,128)(2,1)} %copy-done.18, ...), custom_call_target="tpu_custom_call" | custom-call | flops 1342177280 | bytes 8388608 | tf_op jit(solution)/shard_map/weight_gradient/pallas_call | solution.py:161
  129.0 11.6 %attend_backward.1 = (bf16[1024,256]{1,0:T(8,128)(2,1)}, bf16[1024,256]{1,0:T(8,128)(2,1)}, bf16[1024,256]{1,0:T(8,128)(2,1)}) custom-call(s32[2]{0:T(128)} %copy-done.9, bf16[8,64,2560]{2,1,0:T(8,128)(2,1)} %all-gather.2.cloned.1.call-done.own_ref, bf16[64,2560]{1,0:T(8,128)(2,1)} %copy-done.5, bf16[64,2560]{1,0:T(8,128)(2,1)} %copy-done.17, ...), custom_call_target="tpu_custom_call" | custom-call | flops 3489660928 | bytes 13893632 | tf_op jit(solution)/shard_map/attend_backward/pallas_call | solution.py:225
  140.6 5.6 %reduce-scatter.2.cloned.1.call-done = bf16[128,2560]{1,0:T(8,128)(2,1)} async-done(((bf16[1024,2560]{1,0:T(8,128)(2,1)}), bf16[128,2560]{1,0:T(8,128)(2,1)}) %reduce-scatter.2.cloned.1.call-update) | async-done | bytes 655376 | tf_op jit(solution)/shard_map/reduce_scatter | solution.py:351
  146.1 1.7 %slice.15 = bf16[64,2560]{1,0:T(8,128)(2,1)} slice(bf16[128,2560]{1,0:T(8,128)(2,1)} %reduce-scatter.2.cloned.1.call-done), slice={[64:128], [0:2560]} | slice | bytes 655360 | tf_op jit(solution)/shard_map/slice | solution.py:355
  147.8 2.2 %collective-permute-start.9 = (bf16[64,2560]{1,0:T(8,128)(2,1)}, bf16[64,2560]{1,0:T(8,128)(2,1)}, u32[]{:S(2)}, u32[]{:S(2)}) collective-permute-start(bf16[64,2560]{1,0:T(8,128)(2,1)} %slice.15), channel_id=1, source_target_pairs={{0,8},{1,9},{2,10},{3,11},{4,12},{5,13},{6,14},{7,15},{8,0},{9,1},... | collective-permute-start | bytes 983048 | tf_op jit(solution)/shard_map/ppermute | solution.py:355
  150.0 4.3 %all-to-all-done.3.one_ref.two_ref = bf16[16,32,2560]{2,1,0:T(8,128)(2,1)S(1)} async-done(((bf16[16,32,2560]{2,1,0:T(8,128)(2,1)}), bf16[16,32,2560]{2,1,0:T(8,128)(2,1)S(1)}, u32[]{:S(2)}, u32[]{:S(2)}) %all-to-all-start.3) | async-done | bytes 2621472 | tf_op jit(solution)/shard_map/all_to_all | solution.py:317
  154.3 1.5 copy-done.13
  155.8 4.8 %adam.1 = (bf16[256,2560]{1,0:T(8,128)(2,1)}, bf16[256,2560]{1,0:T(8,128)(2,1)}, bf16[256,2560]{1,0:T(8,128)(2,1)}) custom-call(bf16[256,2560]{1,0:T(8,128)(2,1)} %bitcast.21, bf16[16,32,2560]{2,1,0:T(8,128)(2,1)} %copy-done.13, bf16[16,32,2560]{2,1,0:T(8,128)(2,1)} %copy-done.13, f32[256,2560]{1,0:T(8,128)} %weight_gradient.1.g_ref), custom_call_target="tpu_custom_call" | custom-call | flops 13107200 | bytes 10485760 | tf_op jit(solution)/shard_map/adam/pallas_call | solution.py:274
  160.7 0.0 collective-permute-done.9
  160.7 1.8 %fusion = bf16[1,64,2560]{2,1,0:T(8,128)(2,1)} fusion(bf16[64,2560]{1,0:T(8,128)(2,1)} %collective-permute-done.9, bf16[128,2560]{1,0:T(8,128)(2,1)S(1)} %copy-done.16), kind=kLoop, calls=%fused_computation.2 | loop fusion | flops 655360 | bytes 983040 | tf_op jit(solution)/shard_map/broadcast_in_dim | solution.py:360
  (25 shorter events, 0.1 us)
Async XLA Ops:
  7.2 6.6 %copy-start.19 = (bf16[1,64,2560]{2,1,0:T(8,128)(2,1)S(1)}, bf16[1,64,2560]{2,1,0:T(8,128)(2,1)}, u32[]{:S(2)}) copy-start(bf16[1,64,2560]{2,1,0:T(8,128)(2,1)} %param.12) | copy-start | bytes 983044
  7.2 9.5 %copy-start.10 = (bf16[1,1024,256]{2,1,0:T(8,128)(2,1)S(1)}, bf16[1,1024,256]{2,1,0:T(8,128)(2,1)}, u32[]{:S(2)}) copy-start(bf16[1,1024,256]{2,1,0:T(8,128)(2,1)} %param.9) | copy-start | bytes 1572868
  7.2 9.5 %copy-start.11 = (bf16[1,1024,256]{2,1,0:T(8,128)(2,1)S(1)}, bf16[1,1024,256]{2,1,0:T(8,128)(2,1)}, u32[]{:S(2)}) copy-start(bf16[1,1024,256]{2,1,0:T(8,128)(2,1)} %param.10) | copy-start | bytes 1572868
  7.2 114.8 %all-gather.2.cloned.1.call-start = ((), (), s32[]{:S(2)}) async-start(), calls=%async_computation.6 | async-start | bytes 2949120 | tf_op jit(solution)/shard_map/all_gather | solution.py:329
  7.9 31.0 %all-to-all-start = ((bf16[16,16,2560]{2,1,0:T(8,128)(2,1)}), bf16[16,16,2560]{2,1,0:T(8,128)(2,1)S(1)}, u32[]{:S(2)}, u32[]{:S(2)}) async-start(bf16[16,16,2560]{2,1,0:T(8,128)(2,1)} %bitcast.31), calls=%async_computation | async-start | bytes 2621440 | tf_op jit(solution)/shard_map/all_to_all | solution.py:317
  13.8 25.1 %collective-permute-start = (bf16[64,2560]{1,0:T(8,128)(2,1)S(1)}, bf16[64,2560]{1,0:T(8,128)(2,1)S(1)}, u32[]{:S(2)}, u32[]{:S(2)}) collective-permute-start(bf16[64,2560]{1,0:T(8,128)(2,1)S(1)} %bitcast.32), channel_id=1, source_target_pairs={{0,8},{1,9},{2,10},{3,11},{4,12},{5,13},{6,14},{7,15},{8,0},{9,1},... | collective-permute-start | bytes 983048 | tf_op jit(solution)/shard_map/ppermute | solution.py:333
  16.7 9.3 %copy-start.9 = (s32[2]{0:T(128)}, s32[2]{0:T(128)S(1)}, u32[]{:S(2)}) copy-start(s32[2]{0:T(128)S(1)} %pad_add_fusion.spot_ref) | copy-start | bytes 28
  16.7 1.0 copy-start.12
  17.8 6.5 %copy-start.14 = (bf16[1,256,2560]{2,1,0:T(8,128)(2,1)S(1)}, bf16[1,256,2560]{2,1,0:T(8,128)(2,1)}, u32[]{:S(2)}) copy-start(bf16[1,256,2560]{2,1,0:T(8,128)(2,1)} %param.15) | copy-start | bytes 3932164
  17.8 6.5 %copy-start.15 = (bf16[1,256,2560]{2,1,0:T(8,128)(2,1)S(1)}, bf16[1,256,2560]{2,1,0:T(8,128)(2,1)}, u32[]{:S(2)}) copy-start(bf16[1,256,2560]{2,1,0:T(8,128)(2,1)} %param.14) | copy-start | bytes 3932164
  24.3 47.5 %copy-start.1 = (bf16[16,64,256]{2,1,0:T(8,128)(2,1)}, bf16[16,64,256]{2,1,0:T(8,128)(2,1)S(1)}, u32[]{:S(2)}) copy-start(bf16[16,64,256]{2,1,0:T(8,128)(2,1)S(1)} %get-tuple-element.18.refs_1_.a_ref) | copy-start | bytes 1572868
  24.3 14.6 %copy-start.8 = (s32[16]{0:T(128)S(1)}, s32[16]{0:T(128)}, u32[]{:S(2)}) copy-start(s32[16]{0:T(128)} %source_ref.3) | copy-start | bytes 196
  38.9 9.3 %copy-start.5 = (bf16[64,2560]{1,0:T(8,128)(2,1)}, bf16[64,2560]{1,0:T(8,128)(2,1)S(1)}, u32[]{:S(2)}) copy-start(bf16[64,2560]{1,0:T(8,128)(2,1)S(1)} %collective-permute-done.refs_0_) | copy-start | bytes 983044
  40.7 31.1 %all-to-all-start.1 = ((bf16[16,16,2560]{2,1,0:T(8,128)(2,1)}), bf16[16,16,2560]{2,1,0:T(8,128)(2,1)S(1)}, u32[]{:S(2)}, u32[]{:S(2)}) async-start(bf16[16,16,2560]{2,1,0:T(8,128)(2,1)} %select_pieces.2), calls=%async_computation.1 | async-start | bytes 2621440 | tf_op jit(solution)/shard_map/all_to_all | solution.py:317
  46.2 99.9 %reduce-scatter.2.cloned.1.call-start = ((), (), s32[]{:S(2)}) async-start(), calls=%async_computation.5 | async-start | bytes 5898240 | tf_op jit(solution)/shard_map/reduce_scatter | solution.py:351
  46.2 14.8 %collective-permute-start.1 = (bf16[64,2560]{1,0:T(8,128)(2,1)S(1)}, bf16[64,2560]{1,0:T(8,128)(2,1)S(1)}, u32[]{:S(2)}, u32[]{:S(2)}) collective-permute-start(bf16[64,2560]{1,0:T(8,128)(2,1)S(1)} %collective-permute-done.refs_0_), channel_id=1, source_target_pairs={{0,1},{1,2},{2,3},{3,4},{4,5},{5,6},{6,7},{7,0},{8,9},{9,10},{10,1... | collective-permute-start | bytes 983048 | tf_op jit(solution)/shard_map/ppermute | solution.py:337
  48.2 12.8 %collective-permute-start.3 = (bf16[64,2560]{1,0:T(8,128)(2,1)S(1)}, bf16[64,2560]{1,0:T(8,128)(2,1)S(1)}, u32[]{:S(2)}, u32[]{:S(2)}) collective-permute-start(bf16[64,2560]{1,0:T(8,128)(2,1)S(1)} %collective-permute-done.refs_0_), channel_id=1, source_target_pairs={{0,7},{1,0},{2,1},{3,2},{4,3},{5,4},{6,5},{7,6},{8,15},{9,8},{10,9... | collective-permute-start | bytes 983048 | tf_op jit(solution)/shard_map/ppermute | solution.py:338
  61.0 14.6 %copy-start.17 = (bf16[64,2560]{1,0:T(8,128)(2,1)}, bf16[64,2560]{1,0:T(8,128)(2,1)S(1)}, u32[]{:S(2)}) copy-start(bf16[64,2560]{1,0:T(8,128)(2,1)S(1)} %collective-permute-done.1.refs_1_) | copy-start | bytes 983044
  61.0 10.8 %collective-permute-start.2 = (bf16[64,2560]{1,0:T(8,128)(2,1)S(1)}, bf16[64,2560]{1,0:T(8,128)(2,1)S(1)}, u32[]{:S(2)}, u32[]{:S(2)}) collective-permute-start(bf16[64,2560]{1,0:T(8,128)(2,1)S(1)} %collective-permute-done.1.refs_1_), channel_id=1, source_target_pairs={{0,1},{1,2},{2,3},{3,4},{4,5},{5,6},{6,7},{7,0},{8,9},{9,10},{10,1... | collective-permute-start | bytes 983048 | tf_op jit(solution)/shard_map/ppermute | solution.py:337
  61.0 14.6 %copy-start.18 = (bf16[64,2560]{1,0:T(8,128)(2,1)}, bf16[64,2560]{1,0:T(8,128)(2,1)S(1)}, u32[]{:S(2)}) copy-start(bf16[64,2560]{1,0:T(8,128)(2,1)S(1)} %collective-permute-done.3.refs_2_) | copy-start | bytes 983044
  61.0 10.8 %collective-permute-start.4 = (bf16[64,2560]{1,0:T(8,128)(2,1)S(1)}, bf16[64,2560]{1,0:T(8,128)(2,1)S(1)}, u32[]{:S(2)}, u32[]{:S(2)}) collective-permute-start(bf16[64,2560]{1,0:T(8,128)(2,1)S(1)} %collective-permute-done.3.refs_2_), channel_id=1, source_target_pairs={{0,7},{1,0},{2,1},{3,2},{4,3},{5,4},{6,5},{7,6},{8,15},{9,8},{10,9... | collective-permute-start | bytes 983048 | tf_op jit(solution)/shard_map/ppermute | solution.py:338
  71.8 9.5 %copy-start.6 = (bf16[64,2560]{1,0:T(8,128)(2,1)}, bf16[64,2560]{1,0:T(8,128)(2,1)S(1)}, u32[]{:S(2)}) copy-start(bf16[64,2560]{1,0:T(8,128)(2,1)S(1)} %collective-permute-done.2.refs_0_.refs_3_) | copy-start | bytes 983044
  71.8 9.5 %copy-start.7 = (bf16[64,2560]{1,0:T(8,128)(2,1)}, bf16[64,2560]{1,0:T(8,128)(2,1)S(1)}, u32[]{:S(2)}) copy-start(bf16[64,2560]{1,0:T(8,128)(2,1)S(1)} %collective-permute-done.4.refs_1_.refs_4_) | copy-start | bytes 983044
  71.8 3.8 %copy-start = (bf16[16,16,2560]{2,1,0:T(8,128)(2,1)}, bf16[16,16,2560]{2,1,0:T(8,128)(2,1)S(1)}, u32[]{:S(2)}) copy-start(bf16[16,16,2560]{2,1,0:T(8,128)(2,1)S(1)} %all-to-all-done.1) | copy-start | bytes 3932164
  75.6 37.7 %all-to-all-start.2 = ((bf16[16,32,2560]{2,1,0:T(8,128)(2,1)}), bf16[16,32,2560]{2,1,0:T(8,128)(2,1)}, u32[]{:S(2)}, u32[]{:S(2)}) async-start(bf16[16,32,2560]{2,1,0:T(8,128)(2,1)} %pad_maximum_fusion.refs_2_), calls=%async_computation.3 | async-start | bytes 5242880 | tf_op jit(solution)/shard_map/all_to_all | solution.py:317
  81.2 14.7 %collective-permute-start.5 = (bf16[64,2560]{1,0:T(8,128)(2,1)S(1)}, bf16[64,2560]{1,0:T(8,128)(2,1)S(1)}, u32[]{:S(2)}, u32[]{:S(2)}) collective-permute-start(bf16[64,2560]{1,0:T(8,128)(2,1)S(1)} %collective-permute-done.2.refs_0_.refs_3_), channel_id=1, source_target_pairs={{0,1},{1,2},{2,3},{3,4},{4,5},{5,6},{6,7},{7,0},{8,9},{9,10},{10,1... | collective-permute-start | bytes 983048 | tf_op jit(solution)/shard_map/ppermute | solution.py:337
  81.3 17.3 %collective-permute-start.6 = (bf16[64,2560]{1,0:T(8,128)(2,1)S(1)}, bf16[64,2560]{1,0:T(8,128)(2,1)S(1)}, u32[]{:S(2)}, u32[]{:S(2)}) collective-permute-start(bf16[64,2560]{1,0:T(8,128)(2,1)S(1)} %collective-permute-done.4.refs_1_.refs_4_), channel_id=1, source_target_pairs={{0,7},{1,0},{2,1},{3,2},{4,3},{5,4},{6,5},{7,6},{8,15},{9,8},{10,9... | collective-permute-start | bytes 983048 | tf_op jit(solution)/shard_map/ppermute | solution.py:338
  96.0 20.7 %copy-start.2 = (bf16[64,2560]{1,0:T(8,128)(2,1)}, bf16[64,2560]{1,0:T(8,128)(2,1)S(1)}, u32[]{:S(2)}) copy-start(bf16[64,2560]{1,0:T(8,128)(2,1)S(1)} %collective-permute-done.5.refs_5_.refs_0_) | copy-start | bytes 983044
  96.0 11.0 %collective-permute-start.7 = (bf16[32,2560]{1,0:T(8,128)(2,1)S(1)}, bf16[32,2560]{1,0:T(8,128)(2,1)S(1)}, u32[]{:S(2)}, u32[]{:S(2)}) collective-permute-start(bf16[32,2560]{1,0:T(8,128)(2,1)S(1)} %slice.16), channel_id=1, source_target_pairs={{0,1},{1,2},{2,3},{3,4},{4,5},{5,6},{6,7},{7,0},{8,9},{9,10},{10,1... | collective-permute-start | bytes 491528 | tf_op jit(solution)/shard_map/ppermute | solution.py:341
  98.6 18.1 %copy-start.3 = (bf16[64,2560]{1,0:T(8,128)(2,1)}, bf16[64,2560]{1,0:T(8,128)(2,1)S(1)}, u32[]{:S(2)}) copy-start(bf16[64,2560]{1,0:T(8,128)(2,1)S(1)} %collective-permute-done.6.refs_6_.refs_1_) | copy-start | bytes 983044
  98.6 10.9 %collective-permute-start.8 = (bf16[32,2560]{1,0:T(8,128)(2,1)S(1)}, bf16[32,2560]{1,0:T(8,128)(2,1)S(1)}, u32[]{:S(2)}, u32[]{:S(2)}) collective-permute-start(bf16[32,2560]{1,0:T(8,128)(2,1)S(1)} %slice.17), channel_id=1, source_target_pairs={{0,7},{1,0},{2,1},{3,2},{4,3},{5,4},{6,5},{7,6},{8,15},{9,8},{10,9... | collective-permute-start | bytes 491528 | tf_op jit(solution)/shard_map/ppermute | solution.py:341
  109.5 7.2 %copy-start.4 = (bf16[64,2560]{1,0:T(8,128)(2,1)}, bf16[64,2560]{1,0:T(8,128)(2,1)S(1)}, u32[]{:S(2)}) copy-start(bf16[64,2560]{1,0:T(8,128)(2,1)S(1)} %constant_dynamic-update-slice_fusion.refs_7_.refs_2_) | copy-start | bytes 983044
  116.7 37.6 %all-to-all-start.3 = ((bf16[16,32,2560]{2,1,0:T(8,128)(2,1)}), bf16[16,32,2560]{2,1,0:T(8,128)(2,1)S(1)}, u32[]{:S(2)}, u32[]{:S(2)}) async-start(bf16[16,32,2560]{2,1,0:T(8,128)(2,1)} %select_pieces.3), calls=%async_computation.4 | async-start | bytes 5242880 | tf_op jit(solution)/shard_map/all_to_all | solution.py:317
  147.8 12.8 %copy-start.16 = (bf16[128,2560]{1,0:T(8,128)(2,1)S(1)}, bf16[128,2560]{1,0:T(8,128)(2,1)}, u32[]{:S(2)}) copy-start(bf16[128,2560]{1,0:T(8,128)(2,1)} %reduce-scatter.2.cloned.1.call-done) | copy-start | bytes 1966084
  147.8 12.8 %collective-permute-start.9 = (bf16[64,2560]{1,0:T(8,128)(2,1)}, bf16[64,2560]{1,0:T(8,128)(2,1)}, u32[]{:S(2)}, u32[]{:S(2)}) collective-permute-start(bf16[64,2560]{1,0:T(8,128)(2,1)} %slice.15), channel_id=1, source_target_pairs={{0,8},{1,9},{2,10},{3,11},{4,12},{5,13},{6,14},{7,15},{8,0},{9,1},... | collective-permute-start | bytes 983048 | tf_op jit(solution)/shard_map/ppermute | solution.py:355
  154.3 1.5 copy-start.13
Sparse Core Ops, SparseCore 0:
  9.8 47.4 all-gather.1
  75.7 70.3 reduce-scatter.1

commit v4 on v3

--- a/solution.py
+++ b/solution.py
@@ -13,6 +13,7 @@
 TOK = 1024
 DOUT = 2560
 COLS = 256
+PIECE = COLS // MEMBERS
 CHUNK = TOK // (ZED * HALVES)
 QB = 256
 SCALE = HD ** (-0.5)
@@ -111,7 +112,7 @@
 
 
 def project(attended, weight, after):
-    block = 256
+    block = 512
     return pl.pallas_call(
         project_kernel,
         grid=(TOK // block,),
@@ -170,7 +171,7 @@
         out_specs=pl.BlockSpec((COLS, block), lambda i: (0, i)),
         out_shape=jax.ShapeDtypeStruct((COLS, DOUT), jnp.float32),
         scratch_shapes=[pltpu.VMEM((COLS, TOK), jnp.bfloat16)],
-        compiler_params=params(59400000),
+        compiler_params=params(),
         cost_estimate=cost(2 * TOK * COLS * DOUT, 2 * TOK * (COLS + DOUT) + 4 * COLS * DOUT),
         name="weight_gradient",
     )(spot, attended, gathered, *incoming)
@@ -244,7 +245,7 @@
             pltpu.VMEM((TOK, HD), jnp.float32),
             pltpu.VMEM((TOK, HD), jnp.float32),
         ],
-        compiler_params=params(59400000),
+        compiler_params=params(),
         cost_estimate=cost(
             2 * TOK * COLS * DOUT + 8 * TOK * TOK * COLS, 2 * (TOK * DOUT + COLS * DOUT + 6 * TOK * COLS + heads * TOK * TOK)
         ),
@@ -290,8 +291,9 @@
 
 def select_kernel(source_ref, x_ref, *refs):
     o_ref, sems = refs[-2:]
+    rows = pl.ds(pl.multiple_of(pl.program_id(0) * PIECE, PIECE), PIECE)
     copies = [
-        pltpu.make_async_copy(x_ref.at[source_ref[i]], o_ref.at[i], sems.at[i]) for i in range(MEMBERS)
+        pltpu.make_async_copy(x_ref.at[source_ref[i]], o_ref.at[i, rows], sems.at[i]) for i in range(MEMBERS)
     ]
     for copy in copies:
         copy.start()
@@ -299,15 +301,19 @@
         copy.wait()
 
 
-def select(source, pieces, after, weighed):
+def select(source, pieces, after, weighed, vmem):
     return pl.pallas_call(
         select_kernel,
-        in_specs=[pl.BlockSpec(memory_space=pltpu.SMEM), pl.BlockSpec(memory_space=pltpu.VMEM)]
+        grid=(pieces.shape[1] // PIECE,),
+        in_specs=[
+            pl.BlockSpec(memory_space=pltpu.SMEM),
+            pl.BlockSpec((MEMBERS, PIECE, DOUT), lambda i: (0, i, 0)),
+        ]
         + [ANYWHERE] * len(after),
         out_specs=ANYWHERE,
         out_shape=jax.ShapeDtypeStruct(pieces.shape, pieces.dtype),
         scratch_shapes=[pltpu.SemaphoreType.DMA((MEMBERS,))],
-        compiler_params=params(),
+        compiler_params=params(vmem),
         cost_estimate=cost(0, weighed * pieces.size),
         name="select_pieces",
     )(source, pieces, *after)
@@ -331,7 +337,7 @@
     attended, chances = forward(spot, queries, keys, values, [])
 
     other = lax.ppermute(own, "tp", HALF_SWAP)
-    weight = swap_members(select(source, swap_members(out_weight.reshape(pieces)), [other, attended, moments], 4)).reshape(COLS, DOUT)
+    weight = swap_members(select(source, swap_members(out_weight.reshape(pieces)), [other, attended, moments], 4, VMEM_BYTES)).reshape(COLS, DOUT)
     up, down, incoming = other, other, [other]
     for _ in range(ZED // 2 - 1):
         up = lax.ppermute(up, "tp", ring(1))
@@ -342,7 +348,7 @@
     incoming.append(jnp.concatenate(across, axis=0))
 
     partial = project(attended.reshape(TOK, COLS), weight, incoming[3:5])
-    moments = swap_members(select(source, swap_members(moments), incoming[5:], 4))
+    moments = swap_members(select(source, swap_members(moments), incoming[5:], 4, 61500000))
     gradient = gradient_of(spot, attended, gathered, incoming)
     query_grad, key_grad, value_grad = backward(
         spot, gathered, incoming, weight, queries, keys, values, chances

time: 172 us -> 171 us (level)
  Pallas kernels: 38.9 us -> 35.3 us
  local copies, waits for them, and re-layouts: 4.35 us -> 7.61 us
  waiting for transfers between devices: 64.6 us -> 62.8 us
    unnamed x41 -> x47, local copies, waits for them, and re-layouts: 2.6 us -> 6.58 us
    ppermute x1, waiting for transfers between devices: 12.9 us -> 10.2 us  [on_device(): other = lax.ppermute(own, 'tp', HALF_SWAP)]
    reduce_scatter x1, waiting for transfers between devices: 5.55 us -> 3.27 us  [on_device(): lax.psum_scatter(partial, 'tp', scatter_dimension=0, tiled=True, axis_ind...]
    pallas_call x1, Pallas kernels: 7.03 us -> 5.01 us  [gradient_of(): pl.pallas_call(gradient_kernel, grid=(DOUT // block,), in_specs=[pl.Block...]
    all_to_all x4, waiting for transfers between devices: 8.08 us -> 9.89 us  [swap_members(): lax.all_to_all(pieces, 'member', split_axis=0, concat_axis=0, tiled=True)]
    concatenate x1, other arithmetic: 1.65 us -> 3.39 us  [on_device(): jnp.concatenate([first_moment.reshape(pieces), second_moment.reshape(piec...]
  transfers between devices with their start and end apart: 16 -> 16, of which waited for: 10 -> 11; matrix products, arithmetic and copies ran while one was open for 2% -> 3% of each run, Pallas kernels for 23% -> 21%
where the time goes in v4:
time: 171 us; the launch traced here: 169 us
  waiting for transfers between devices  62.8 us (37%)
  starting transfers between devices  44.7 us (26%)
  Pallas kernels  35.3 us (21%)
  between operations  14.3 us (8%)
  local copies, waits for them, and re-layouts  7.61 us (4%)
  other arithmetic  4.27 us (2%)
    ppermute x3, waiting for transfers between devices, on_device(): up = lax.ppermute(up, 'tp', ring(1))  27.7 us
    all_to_all x4, starting transfers between devices, swap_members(): lax.all_to_all(pieces, 'member', split_axis=0, concat_axis=0, tiled=True)  23.2 us
    ppermute x3, starting transfers between devices, on_device(): down = lax.ppermute(down, 'tp', ring(-1))  10.5 us
    pallas_call x1, Pallas kernels, backward(): pl.pallas_call(backward_kernel, grid=(heads,), in_specs=[pl.BlockSpec(mem...  10.2 us
    ppermute x1, waiting for transfers between devices, on_device(): other = lax.ppermute(own, 'tp', HALF_SWAP)  10.2 us
    all_to_all x4, waiting for transfers between devices, swap_members(): lax.all_to_all(pieces, 'member', split_axis=0, concat_axis=0, tiled=True)  9.89 us
    unnamed x47, local copies, waits for them, and re-layouts  6.58 us
    pallas_call x1, Pallas kernels, forward(): pl.pallas_call(forward_kernel, grid=(heads,), in_specs=[pl.BlockSpec(memo...  6.54 us
  transfers between devices with their start and end apart: 16, of which 11 were waited for; matrix products, arithmetic and copies ran while one was open for 3% of the time, Pallas kernels for 21%

profile of v4, /device:TPU:8, one launch (start us, length us, event | category | flops | bytes accessed | tf_op | source)
XLA Modules:
  0.0 168.9 jit_solution(9359556280751337191)
XLA Ops:
  7.2 0.0 copy-start.15
  7.2 0.0 all-gather.2.cloned.1.call-start
  7.2 0.7 all-gather.2.cloned.1.call-update
  7.9 5.9 %all-to-all-start = ((bf16[16,16,2560]{2,1,0:T(8,128)(2,1)}), bf16[16,16,2560]{2,1,0:T(8,128)(2,1)S(1)}, u32[]{:S(2)}, u32[]{:S(2)}) async-start(bf16[16,16,2560]{2,1,0:T(8,128)(2,1)} %bitcast.31), calls=%async_computation | async-start | bytes 2621440 | tf_op jit(solution)/shard_map/all_to_all | solution.py:323
  13.8 2.8 %collective-permute-start = (bf16[64,2560]{1,0:T(8,128)(2,1)S(1)}, bf16[64,2560]{1,0:T(8,128)(2,1)S(1)}, u32[]{:S(2)}, u32[]{:S(2)}) collective-permute-start(bf16[64,2560]{1,0:T(8,128)(2,1)S(1)} %bitcast.32), channel_id=1, source_target_pairs={{0,8},{1,9},{2,10},{3,11},{4,12},{5,13},{6,14},{7,15},{8,0},{9,1},... | collective-permute-start | bytes 983048 | tf_op jit(solution)/shard_map/ppermute | solution.py:339
  16.6 0.1 pad_add_fusion.spot_ref
  16.7 1.0 copy-done.17
  17.7 1.0 copy-done.19
  18.8 6.5 %attend_forward.1 = (bf16[16,64,256]{2,1,0:T(8,128)(2,1)S(1)}, bf16[2,1024,1024]{2,1,0:T(8,128)(2,1)}) custom-call(s32[2]{0:T(128)S(1)} %pad_add_fusion.spot_ref, bf16[1024,256]{1,0:T(8,128)(2,1)S(1)} %bitcast.23, bf16[1024,256]{1,0:T(8,128)(2,1)S(1)} %bitcast.25, bf16[1024,256]{1,0:T(8,128)(2,1)S(1)} %bitcast.27), custom_call_target="tpu_custom_call" | custom-call | flops 1073741824 | bytes 6291456 | tf_op jit(solution)/shard_map/attend_forward/pallas_call | solution.py:91
  25.3 3.4 %pad_maximum_fusion.refs_2_ = bf16[16,32,2560]{2,1,0:T(8,128)(2,1)} fusion(bf16[16,16,2560]{2,1,0:T(8,128)(2,1)} %bitcast.29, bf16[16,16,2560]{2,1,0:T(8,128)(2,1)} %bitcast.30), kind=kLoop, calls=%fused_computation | loop fusion | flops 5242880 | bytes 5242880 | tf_op jit(solution)/shard_map/concatenate | solution.py:336
  28.7 10.2 %collective-permute-done.refs_0_ = bf16[64,2560]{1,0:T(8,128)(2,1)S(1)} collective-permute-done((bf16[64,2560]{1,0:T(8,128)(2,1)S(1)}, bf16[64,2560]{1,0:T(8,128)(2,1)S(1)}, u32[]{:S(2)}, u32[]{:S(2)}) %collective-permute-start) | collective-permute-done | bytes 327712 | tf_op jit(solution)/shard_map/ppermute | solution.py:339
  38.9 0.0 all-to-all-done.x_ref
  38.9 1.7 %select_pieces.2 = bf16[16,16,2560]{2,1,0:T(8,128)(2,1)} custom-call(s32[16]{0:T(128)S(1)} %copy-done.14, bf16[16,16,2560]{2,1,0:T(8,128)(2,1)S(1)} %all-to-all-done.x_ref, bf16[64,2560]{1,0:T(8,128)(2,1)S(1)} %collective-permute-done.refs_0_, bf16[16,64,256]{2,1,0:T(8,128)(2,1)S(1)} %get-tuple-element.18.refs_1_.a_ref, ...), custom_call_target="tpu_custom_call" | custom-call | bytes 2621440 | tf_op jit(solution)/shard_map/select_pieces/pallas_call | solution.py:305
  40.6 5.5 %all-to-all-start.1 = ((bf16[16,16,2560]{2,1,0:T(8,128)(2,1)}), bf16[16,16,2560]{2,1,0:T(8,128)(2,1)S(1)}, u32[]{:S(2)}, u32[]{:S(2)}) async-start(bf16[16,16,2560]{2,1,0:T(8,128)(2,1)} %select_pieces.2), calls=%async_computation.1 | async-start | bytes 2621440 | tf_op jit(solution)/shard_map/all_to_all | solution.py:323
  46.1 0.0 reduce-scatter.2.cloned.1.call-start
  46.1 2.0 %collective-permute-start.1 = (bf16[64,2560]{1,0:T(8,128)(2,1)S(1)}, bf16[64,2560]{1,0:T(8,128)(2,1)S(1)}, u32[]{:S(2)}, u32[]{:S(2)}) collective-permute-start(bf16[64,2560]{1,0:T(8,128)(2,1)S(1)} %collective-permute-done.refs_0_), channel_id=1, source_target_pairs={{0,1},{1,2},{2,3},{3,4},{4,5},{5,6},{6,7},{7,0},{8,9},{9,10},{10,1... | collective-permute-start | bytes 983048 | tf_op jit(solution)/shard_map/ppermute | solution.py:343
  48.1 4.0 %collective-permute-start.3 = (bf16[64,2560]{1,0:T(8,128)(2,1)S(1)}, bf16[64,2560]{1,0:T(8,128)(2,1)S(1)}, u32[]{:S(2)}, u32[]{:S(2)}) collective-permute-start(bf16[64,2560]{1,0:T(8,128)(2,1)S(1)} %collective-permute-done.refs_0_), channel_id=1, source_target_pairs={{0,7},{1,0},{2,1},{3,2},{4,3},{5,4},{6,5},{7,6},{8,15},{9,8},{10,9... | collective-permute-start | bytes 983048 | tf_op jit(solution)/shard_map/ppermute | solution.py:344
  52.2 8.8 %collective-permute-done.1.refs_1_ = bf16[64,2560]{1,0:T(8,128)(2,1)S(1)} collective-permute-done((bf16[64,2560]{1,0:T(8,128)(2,1)S(1)}, bf16[64,2560]{1,0:T(8,128)(2,1)S(1)}, u32[]{:S(2)}, u32[]{:S(2)}) %collective-permute-start.1) | collective-permute-done | bytes 327712 | tf_op jit(solution)/shard_map/ppermute | solution.py:343
  60.9 0.0 collective-permute-start.2
  60.9 0.0 collective-permute-done.3.refs_2_
  60.9 0.0 copy-start.12
  61.0 3.2 %collective-permute-start.4 = (bf16[64,2560]{1,0:T(8,128)(2,1)S(1)}, bf16[64,2560]{1,0:T(8,128)(2,1)S(1)}, u32[]{:S(2)}, u32[]{:S(2)}) collective-permute-start(bf16[64,2560]{1,0:T(8,128)(2,1)S(1)} %collective-permute-done.3.refs_2_), channel_id=1, source_target_pairs={{0,7},{1,0},{2,1},{3,2},{4,3},{5,4},{6,5},{7,6},{8,15},{9,8},{10,9... | collective-permute-start | bytes 983048 | tf_op jit(solution)/shard_map/ppermute | solution.py:344
  64.2 7.6 %collective-permute-done.2.refs_0_.refs_3_ = bf16[64,2560]{1,0:T(8,128)(2,1)S(1)} collective-permute-done((bf16[64,2560]{1,0:T(8,128)(2,1)S(1)}, bf16[64,2560]{1,0:T(8,128)(2,1)S(1)}, u32[]{:S(2)}, u32[]{:S(2)}) %collective-permute-start.2) | collective-permute-done | bytes 327712 | tf_op jit(solution)/shard_map/ppermute | solution.py:343
  71.7 0.0 collective-permute-done.4.refs_1_.refs_4_
  71.7 0.0 all-to-all-done.1
  71.7 0.0 copy-start
  71.8 3.2 %project.1 = bf16[1024,2560]{1,0:T(8,128)(2,1)} custom-call(bf16[1024,256]{1,0:T(8,128)(2,1)S(1)} %bitcast.22, bf16[256,2560]{1,0:T(8,128)(2,1)S(1)} %bitcast.19, bf16[64,2560]{1,0:T(8,128)(2,1)S(1)} %collective-permute-done.2.refs_0_.refs_3_, bf16[64,2560]{1,0:T(8,128)(2,1)S(1)} %collective-permute-done.4.refs_1_.refs_4_), custom_call_target="tpu_custom_call" | custom-call | flops 1342177280 | bytes 7077888 | tf_op jit(solution)/shard_map/project/pallas_call | solution.py:116
  75.0 0.0 copy-done.12
  75.0 0.0 reduce-scatter.2.cloned.1.call-update
  75.0 5.8 %all-to-all-start.2 = ((bf16[16,32,2560]{2,1,0:T(8,128)(2,1)}), bf16[16,32,2560]{2,1,0:T(8,128)(2,1)}, u32[]{:S(2)}, u32[]{:S(2)}) async-start(bf16[16,32,2560]{2,1,0:T(8,128)(2,1)} %pad_maximum_fusion.refs_2_), calls=%async_computation.3 | async-start | bytes 5242880 | tf_op jit(solution)/shard_map/all_to_all | solution.py:323
  80.8 0.0 collective-permute-start.5
  80.8 3.2 %collective-permute-start.6 = (bf16[64,2560]{1,0:T(8,128)(2,1)S(1)}, bf16[64,2560]{1,0:T(8,128)(2,1)S(1)}, u32[]{:S(2)}, u32[]{:S(2)}) collective-permute-start(bf16[64,2560]{1,0:T(8,128)(2,1)S(1)} %collective-permute-done.4.refs_1_.refs_4_), channel_id=1, source_target_pairs={{0,7},{1,0},{2,1},{3,2},{4,3},{5,4},{6,5},{7,6},{8,15},{9,8},{10,9... | collective-permute-start | bytes 983048 | tf_op jit(solution)/shard_map/ppermute | solution.py:344
  84.1 11.4 %collective-permute-done.5.refs_5_.refs_0_ = bf16[64,2560]{1,0:T(8,128)(2,1)S(1)} collective-permute-done((bf16[64,2560]{1,0:T(8,128)(2,1)S(1)}, bf16[64,2560]{1,0:T(8,128)(2,1)S(1)}, u32[]{:S(2)}, u32[]{:S(2)}) %collective-permute-start.5) | collective-permute-done | bytes 327712 | tf_op jit(solution)/shard_map/ppermute | solution.py:343
  95.5 0.1 collective-permute-start.7
  95.6 2.6 %collective-permute-done.6.refs_6_.refs_1_ = bf16[64,2560]{1,0:T(8,128)(2,1)S(1)} collective-permute-done((bf16[64,2560]{1,0:T(8,128)(2,1)S(1)}, bf16[64,2560]{1,0:T(8,128)(2,1)S(1)}, u32[]{:S(2)}, u32[]{:S(2)}) %collective-permute-start.6) | collective-permute-done | bytes 327712 | tf_op jit(solution)/shard_map/ppermute | solution.py:344
  98.2 3.8 %collective-permute-start.8 = (bf16[32,2560]{1,0:T(8,128)(2,1)S(1)}, bf16[32,2560]{1,0:T(8,128)(2,1)S(1)}, u32[]{:S(2)}, u32[]{:S(2)}) collective-permute-start(bf16[32,2560]{1,0:T(8,128)(2,1)S(1)} %slice.17), channel_id=1, source_target_pairs={{0,7},{1,0},{2,1},{3,2},{4,3},{5,4},{6,5},{7,6},{8,15},{9,8},{10,9... | collective-permute-start | bytes 491528 | tf_op jit(solution)/shard_map/ppermute | solution.py:347
  101.9 4.5 %collective-permute-done.7 = bf16[32,2560]{1,0:T(8,128)(2,1)S(1)} collective-permute-done((bf16[32,2560]{1,0:T(8,128)(2,1)S(1)}, bf16[32,2560]{1,0:T(8,128)(2,1)S(1)}, u32[]{:S(2)}, u32[]{:S(2)}) %collective-permute-start.7) | collective-permute-done | bytes 163872 | tf_op jit(solution)/shard_map/ppermute | solution.py:347
  106.5 2.6 %collective-permute-done.8 = bf16[32,2560]{1,0:T(8,128)(2,1)S(1)} collective-permute-done((bf16[32,2560]{1,0:T(8,128)(2,1)S(1)}, bf16[32,2560]{1,0:T(8,128)(2,1)S(1)}, u32[]{:S(2)}, u32[]{:S(2)}) %collective-permute-start.8) | collective-permute-done | bytes 163872 | tf_op jit(solution)/shard_map/ppermute | solution.py:347
  109.1 0.0 copy-start.6
  109.1 3.7 %all-to-all-done.2.x_ref = bf16[16,32,2560]{2,1,0:T(8,128)(2,1)} async-done(((bf16[16,32,2560]{2,1,0:T(8,128)(2,1)}), bf16[16,32,2560]{2,1,0:T(8,128)(2,1)}, u32[]{:S(2)}, u32[]{:S(2)}) %all-to-all-start.2) | async-done | bytes 2621472 | tf_op jit(solution)/shard_map/all_to_all | solution.py:323
  112.9 3.7 %select_pieces.3 = bf16[16,32,2560]{2,1,0:T(8,128)(2,1)} custom-call(s32[16]{0:T(128)} %source_ref.3, bf16[16,32,2560]{2,1,0:T(8,128)(2,1)} %all-to-all-done.2.x_ref, bf16[64,2560]{1,0:T(8,128)(2,1)} %copy-done.2, bf16[64,2560]{1,0:T(8,128)(2,1)} %copy-done.4, bf16[64,2560]{1,0:T(8,128)(2,1)} %copy-done.6), custom_call_target="tpu_custom_call" | custom-call | bytes 5242880 | tf_op jit(solution)/shard_map/select_pieces/pallas_call | solution.py:305
  116.5 0.0 copy-start.3
  116.6 0.0 copy-start.5
  116.6 0.0 copy-start.7
  116.6 6.0 %all-to-all-start.3 = ((bf16[16,32,2560]{2,1,0:T(8,128)(2,1)}), bf16[16,32,2560]{2,1,0:T(8,128)(2,1)}, u32[]{:S(2)}, u32[]{:S(2)}) async-start(bf16[16,32,2560]{2,1,0:T(8,128)(2,1)} %select_pieces.3), calls=%async_computation.4 | async-start | bytes 5242880 | tf_op jit(solution)/shard_map/all_to_all | solution.py:323
  122.6 0.0 all-gather.2.cloned.1.call-done.own_ref
  122.6 0.0 copy-done.3
  122.6 0.0 copy-done.5
  122.7 0.0 copy-done.7
  122.7 0.0 copy-start.9
  122.7 1.0 copy-done.9
  123.7 1.0 copy-done.11
  124.6 1.0 copy-done.13
  125.6 5.0 %weight_gradient.1.g_ref = f32[256,2560]{1,0:T(8,128)S(1)} custom-call(s32[2]{0:T(128)S(1)} %pad_add_fusion.spot_ref, bf16[16,64,256]{2,1,0:T(8,128)(2,1)S(1)} %get-tuple-element.18.refs_1_.a_ref, bf16[8,64,2560]{2,1,0:T(8,128)(2,1)} %all-gather.2.cloned.1.call-done.own_ref, bf16[64,2560]{1,0:T(8,128)(2,1)S(1)} %collective-permute-done.refs_0_, ...), custom_call_target="tpu_custom_call" | custom-call | flops 1342177280 | bytes 8388608 | tf_op jit(solution)/shard_map/weight_gradient/pallas_call | solution.py:162
  130.6 1.5 copy-done.1
  132.1 0.0 copy-done.16
  132.1 10.2 %attend_backward.1 = (bf16[1024,256]{1,0:T(8,128)(2,1)}, bf16[1024,256]{1,0:T(8,128)(2,1)}, bf16[1024,256]{1,0:T(8,128)(2,1)}) custom-call(s32[2]{0:T(128)S(1)} %pad_add_fusion.spot_ref, bf16[8,64,2560]{2,1,0:T(8,128)(2,1)} %all-gather.2.cloned.1.call-done.own_ref, bf16[64,2560]{1,0:T(8,128)(2,1)S(1)} %collective-permute-done.refs_0_, ...), custom_call_target="tpu_custom_call" | custom-call | flops 3489660928 | bytes 13893632 | tf_op jit(solution)/shard_map/attend_backward/pallas_call | solution.py:226
  142.3 3.3 %reduce-scatter.2.cloned.1.call-done = bf16[128,2560]{1,0:T(8,128)(2,1)} async-done(((bf16[1024,2560]{1,0:T(8,128)(2,1)}), bf16[128,2560]{1,0:T(8,128)(2,1)}) %reduce-scatter.2.cloned.1.call-update) | async-done | bytes 655376 | tf_op jit(solution)/shard_map/reduce_scatter | solution.py:357
  145.6 1.0 slice.15
  146.6 2.3 %collective-permute-start.9 = (bf16[64,2560]{1,0:T(8,128)(2,1)S(1)}, bf16[64,2560]{1,0:T(8,128)(2,1)S(1)}, u32[]{:S(2)}, u32[]{:S(2)}) collective-permute-start(bf16[64,2560]{1,0:T(8,128)(2,1)S(1)} %slice.15), channel_id=1, source_target_pairs={{0,8},{1,9},{2,10},{3,11},{4,12},{5,13},{6,14},{7,15},{8,0},{9,1},... | collective-permute-start | bytes 983048 | tf_op jit(solution)/shard_map/ppermute | solution.py:361
  148.9 6.2 %all-to-all-done.3.one_ref.two_ref = bf16[16,32,2560]{2,1,0:T(8,128)(2,1)} async-done(((bf16[16,32,2560]{2,1,0:T(8,128)(2,1)}), bf16[16,32,2560]{2,1,0:T(8,128)(2,1)}, u32[]{:S(2)}, u32[]{:S(2)}) %all-to-all-start.3) | async-done | bytes 2621472 | tf_op jit(solution)/shard_map/all_to_all | solution.py:323
  155.1 4.8 %adam.1 = (bf16[256,2560]{1,0:T(8,128)(2,1)}, bf16[256,2560]{1,0:T(8,128)(2,1)}, bf16[256,2560]{1,0:T(8,128)(2,1)}) custom-call(bf16[256,2560]{1,0:T(8,128)(2,1)} %bitcast.21, bf16[16,32,2560]{2,1,0:T(8,128)(2,1)} %all-to-all-done.3.one_ref.two_ref, bf16[16,32,2560]{2,1,0:T(8,128)(2,1)} %all-to-all-done.3.one_ref.two_ref, f32[256,2560]{1,0:T(8,128)} %copy-done.1), custom_call_target="tpu_custom_call" | custom-call | flops 13107200 | bytes 10485760 | tf_op jit(solution)/shard_map/adam/pallas_call | solution.py:275
  160.0 1.3 collective-permute-done.9
  161.3 0.8 fusion
  (31 shorter events, 0.1 us)
Async XLA Ops:
  7.2 6.6 %copy-start.22 = (bf16[1,64,2560]{2,1,0:T(8,128)(2,1)S(1)}, bf16[1,64,2560]{2,1,0:T(8,128)(2,1)}, u32[]{:S(2)}) copy-start(bf16[1,64,2560]{2,1,0:T(8,128)(2,1)} %param.12) | copy-start | bytes 983044
  7.2 9.5 %copy-start.15 = (bf16[1,1024,256]{2,1,0:T(8,128)(2,1)S(1)}, bf16[1,1024,256]{2,1,0:T(8,128)(2,1)}, u32[]{:S(2)}) copy-start(bf16[1,1024,256]{2,1,0:T(8,128)(2,1)} %param.9) | copy-start | bytes 1572868
  7.2 115.4 %all-gather.2.cloned.1.call-start = ((), (), s32[]{:S(2)}) async-start(), calls=%async_computation.6 | async-start | bytes 2949120 | tf_op jit(solution)/shard_map/all_gather | solution.py:335
  7.9 31.0 %all-to-all-start = ((bf16[16,16,2560]{2,1,0:T(8,128)(2,1)}), bf16[16,16,2560]{2,1,0:T(8,128)(2,1)S(1)}, u32[]{:S(2)}, u32[]{:S(2)}) async-start(bf16[16,16,2560]{2,1,0:T(8,128)(2,1)} %bitcast.31), calls=%async_computation | async-start | bytes 2621440 | tf_op jit(solution)/shard_map/all_to_all | solution.py:323
  13.8 25.1 %collective-permute-start = (bf16[64,2560]{1,0:T(8,128)(2,1)S(1)}, bf16[64,2560]{1,0:T(8,128)(2,1)S(1)}, u32[]{:S(2)}, u32[]{:S(2)}) collective-permute-start(bf16[64,2560]{1,0:T(8,128)(2,1)S(1)} %bitcast.32), channel_id=1, source_target_pairs={{0,8},{1,9},{2,10},{3,11},{4,12},{5,13},{6,14},{7,15},{8,0},{9,1},... | collective-permute-start | bytes 983048 | tf_op jit(solution)/shard_map/ppermute | solution.py:339
  16.7 1.0 copy-start.17
  17.7 1.0 copy-start.19
  25.3 13.6 %copy-start.14 = (s32[16]{0:T(128)S(1)}, s32[16]{0:T(128)}, u32[]{:S(2)}) copy-start(s32[16]{0:T(128)} %source_ref.3) | copy-start | bytes 196
  40.6 31.1 %all-to-all-start.1 = ((bf16[16,16,2560]{2,1,0:T(8,128)(2,1)}), bf16[16,16,2560]{2,1,0:T(8,128)(2,1)S(1)}, u32[]{:S(2)}, u32[]{:S(2)}) async-start(bf16[16,16,2560]{2,1,0:T(8,128)(2,1)} %select_pieces.2), calls=%async_computation.1 | async-start | bytes 2621440 | tf_op jit(solution)/shard_map/all_to_all | solution.py:323
  46.1 99.5 %reduce-scatter.2.cloned.1.call-start = ((), (), s32[]{:S(2)}) async-start(), calls=%async_computation.5 | async-start | bytes 5898240 | tf_op jit(solution)/shard_map/reduce_scatter | solution.py:357
  46.1 14.8 %collective-permute-start.1 = (bf16[64,2560]{1,0:T(8,128)(2,1)S(1)}, bf16[64,2560]{1,0:T(8,128)(2,1)S(1)}, u32[]{:S(2)}, u32[]{:S(2)}) collective-permute-start(bf16[64,2560]{1,0:T(8,128)(2,1)S(1)} %collective-permute-done.refs_0_), channel_id=1, source_target_pairs={{0,1},{1,2},{2,3},{3,4},{4,5},{5,6},{6,7},{7,0},{8,9},{9,10},{10,1... | collective-permute-start | bytes 983048 | tf_op jit(solution)/shard_map/ppermute | solution.py:343
  48.1 12.8 %collective-permute-start.3 = (bf16[64,2560]{1,0:T(8,128)(2,1)S(1)}, bf16[64,2560]{1,0:T(8,128)(2,1)S(1)}, u32[]{:S(2)}, u32[]{:S(2)}) collective-permute-start(bf16[64,2560]{1,0:T(8,128)(2,1)S(1)} %collective-permute-done.refs_0_), channel_id=1, source_target_pairs={{0,7},{1,0},{2,1},{3,2},{4,3},{5,4},{6,5},{7,6},{8,15},{9,8},{10,9... | collective-permute-start | bytes 983048 | tf_op jit(solution)/shard_map/ppermute | solution.py:344
  60.9 14.1 %copy-start.10 = (bf16[64,2560]{1,0:T(8,128)(2,1)}, bf16[64,2560]{1,0:T(8,128)(2,1)S(1)}, u32[]{:S(2)}) copy-start(bf16[64,2560]{1,0:T(8,128)(2,1)S(1)} %collective-permute-done.1.refs_1_) | copy-start | bytes 983044
  60.9 10.8 %collective-permute-start.2 = (bf16[64,2560]{1,0:T(8,128)(2,1)S(1)}, bf16[64,2560]{1,0:T(8,128)(2,1)S(1)}, u32[]{:S(2)}, u32[]{:S(2)}) collective-permute-start(bf16[64,2560]{1,0:T(8,128)(2,1)S(1)} %collective-permute-done.1.refs_1_), channel_id=1, source_target_pairs={{0,1},{1,2},{2,3},{3,4},{4,5},{5,6},{6,7},{7,0},{8,9},{9,10},{10,1... | collective-permute-start | bytes 983048 | tf_op jit(solution)/shard_map/ppermute | solution.py:343
  60.9 14.1 %copy-start.12 = (bf16[64,2560]{1,0:T(8,128)(2,1)}, bf16[64,2560]{1,0:T(8,128)(2,1)S(1)}, u32[]{:S(2)}) copy-start(bf16[64,2560]{1,0:T(8,128)(2,1)S(1)} %collective-permute-done.3.refs_2_) | copy-start | bytes 983044
  61.0 10.8 %collective-permute-start.4 = (bf16[64,2560]{1,0:T(8,128)(2,1)S(1)}, bf16[64,2560]{1,0:T(8,128)(2,1)S(1)}, u32[]{:S(2)}, u32[]{:S(2)}) collective-permute-start(bf16[64,2560]{1,0:T(8,128)(2,1)S(1)} %collective-permute-done.3.refs_2_), channel_id=1, source_target_pairs={{0,7},{1,0},{2,1},{3,2},{4,3},{5,4},{6,5},{7,6},{8,15},{9,8},{10,9... | collective-permute-start | bytes 983048 | tf_op jit(solution)/shard_map/ppermute | solution.py:344
  71.7 9.1 %copy-start.8 = (bf16[64,2560]{1,0:T(8,128)(2,1)}, bf16[64,2560]{1,0:T(8,128)(2,1)S(1)}, u32[]{:S(2)}) copy-start(bf16[64,2560]{1,0:T(8,128)(2,1)S(1)} %collective-permute-done.4.refs_1_.refs_4_) | copy-start | bytes 983044
  71.7 60.4 %copy-start = (bf16[16,16,2560]{2,1,0:T(8,128)(2,1)}, bf16[16,16,2560]{2,1,0:T(8,128)(2,1)S(1)}, u32[]{:S(2)}) copy-start(bf16[16,16,2560]{2,1,0:T(8,128)(2,1)S(1)} %all-to-all-done.1) | copy-start | bytes 3932164
  75.0 37.8 %all-to-all-start.2 = ((bf16[16,32,2560]{2,1,0:T(8,128)(2,1)}), bf16[16,32,2560]{2,1,0:T(8,128)(2,1)}, u32[]{:S(2)}, u32[]{:S(2)}) async-start(bf16[16,32,2560]{2,1,0:T(8,128)(2,1)} %pad_maximum_fusion.refs_2_), calls=%async_computation.3 | async-start | bytes 5242880 | tf_op jit(solution)/shard_map/all_to_all | solution.py:323
  80.8 14.7 %collective-permute-start.5 = (bf16[64,2560]{1,0:T(8,128)(2,1)S(1)}, bf16[64,2560]{1,0:T(8,128)(2,1)S(1)}, u32[]{:S(2)}, u32[]{:S(2)}) collective-permute-start(bf16[64,2560]{1,0:T(8,128)(2,1)S(1)} %collective-permute-done.2.refs_0_.refs_3_), channel_id=1, source_target_pairs={{0,1},{1,2},{2,3},{3,4},{4,5},{5,6},{6,7},{7,0},{8,9},{9,10},{10,1... | collective-permute-start | bytes 983048 | tf_op jit(solution)/shard_map/ppermute | solution.py:343
  80.8 17.3 %collective-permute-start.6 = (bf16[64,2560]{1,0:T(8,128)(2,1)S(1)}, bf16[64,2560]{1,0:T(8,128)(2,1)S(1)}, u32[]{:S(2)}, u32[]{:S(2)}) collective-permute-start(bf16[64,2560]{1,0:T(8,128)(2,1)S(1)} %collective-permute-done.4.refs_1_.refs_4_), channel_id=1, source_target_pairs={{0,7},{1,0},{2,1},{3,2},{4,3},{5,4},{6,5},{7,6},{8,15},{9,8},{10,9... | collective-permute-start | bytes 983048 | tf_op jit(solution)/shard_map/ppermute | solution.py:344
  95.5 17.4 %copy-start.2 = (bf16[64,2560]{1,0:T(8,128)(2,1)}, bf16[64,2560]{1,0:T(8,128)(2,1)S(1)}, u32[]{:S(2)}) copy-start(bf16[64,2560]{1,0:T(8,128)(2,1)S(1)} %collective-permute-done.5.refs_5_.refs_0_) | copy-start | bytes 983044
  95.5 11.0 %collective-permute-start.7 = (bf16[32,2560]{1,0:T(8,128)(2,1)S(1)}, bf16[32,2560]{1,0:T(8,128)(2,1)S(1)}, u32[]{:S(2)}, u32[]{:S(2)}) collective-permute-start(bf16[32,2560]{1,0:T(8,128)(2,1)S(1)} %slice.16), channel_id=1, source_target_pairs={{0,1},{1,2},{2,3},{3,4},{4,5},{5,6},{6,7},{7,0},{8,9},{9,10},{10,1... | collective-permute-start | bytes 491528 | tf_op jit(solution)/shard_map/ppermute | solution.py:347
  98.2 14.7 %copy-start.4 = (bf16[64,2560]{1,0:T(8,128)(2,1)}, bf16[64,2560]{1,0:T(8,128)(2,1)S(1)}, u32[]{:S(2)}) copy-start(bf16[64,2560]{1,0:T(8,128)(2,1)S(1)} %collective-permute-done.6.refs_6_.refs_1_) | copy-start | bytes 983044
  98.2 10.9 %collective-permute-start.8 = (bf16[32,2560]{1,0:T(8,128)(2,1)S(1)}, bf16[32,2560]{1,0:T(8,128)(2,1)S(1)}, u32[]{:S(2)}, u32[]{:S(2)}) collective-permute-start(bf16[32,2560]{1,0:T(8,128)(2,1)S(1)} %slice.17), channel_id=1, source_target_pairs={{0,7},{1,0},{2,1},{3,2},{4,3},{5,4},{6,5},{7,6},{8,15},{9,8},{10,9... | collective-permute-start | bytes 491528 | tf_op jit(solution)/shard_map/ppermute | solution.py:347
  109.1 3.7 %copy-start.6 = (bf16[64,2560]{1,0:T(8,128)(2,1)}, bf16[64,2560]{1,0:T(8,128)(2,1)S(1)}, u32[]{:S(2)}) copy-start(bf16[64,2560]{1,0:T(8,128)(2,1)S(1)} %constant_dynamic-update-slice_fusion.refs_7_.refs_2_) | copy-start | bytes 983044
  116.5 6.1 %copy-start.3 = (bf16[64,2560]{1,0:T(8,128)(2,1)S(1)}, bf16[64,2560]{1,0:T(8,128)(2,1)}, u32[]{:S(2)}) copy-start(bf16[64,2560]{1,0:T(8,128)(2,1)} %copy-done.2) | copy-start | bytes 983044
  116.6 6.1 %copy-start.5 = (bf16[64,2560]{1,0:T(8,128)(2,1)S(1)}, bf16[64,2560]{1,0:T(8,128)(2,1)}, u32[]{:S(2)}) copy-start(bf16[64,2560]{1,0:T(8,128)(2,1)} %copy-done.4) | copy-start | bytes 983044
  116.6 6.1 %copy-start.7 = (bf16[64,2560]{1,0:T(8,128)(2,1)S(1)}, bf16[64,2560]{1,0:T(8,128)(2,1)}, u32[]{:S(2)}) copy-start(bf16[64,2560]{1,0:T(8,128)(2,1)} %copy-done.6) | copy-start | bytes 983044
  116.6 38.5 %all-to-all-start.3 = ((bf16[16,32,2560]{2,1,0:T(8,128)(2,1)}), bf16[16,32,2560]{2,1,0:T(8,128)(2,1)}, u32[]{:S(2)}, u32[]{:S(2)}) async-start(bf16[16,32,2560]{2,1,0:T(8,128)(2,1)} %select_pieces.3), calls=%async_computation.4 | async-start | bytes 5242880 | tf_op jit(solution)/shard_map/all_to_all | solution.py:323
  122.7 1.0 copy-start.9
  123.6 1.0 copy-start.11
  124.6 1.0 copy-start.13
  125.6 6.5 %copy-start.16 = (bf16[1,1024,256]{2,1,0:T(8,128)(2,1)S(1)}, bf16[1,1024,256]{2,1,0:T(8,128)(2,1)}, u32[]{:S(2)}) copy-start(bf16[1,1024,256]{2,1,0:T(8,128)(2,1)} %param.9) | copy-start | bytes 1572868
  125.6 6.5 %copy-start.18 = (bf16[1,1024,256]{2,1,0:T(8,128)(2,1)S(1)}, bf16[1,1024,256]{2,1,0:T(8,128)(2,1)}, u32[]{:S(2)}) copy-start(bf16[1,1024,256]{2,1,0:T(8,128)(2,1)} %param.10) | copy-start | bytes 1572868
  125.6 6.5 %copy-start.20 = (bf16[1,1024,256]{2,1,0:T(8,128)(2,1)S(1)}, bf16[1,1024,256]{2,1,0:T(8,128)(2,1)}, u32[]{:S(2)}) copy-start(bf16[1,1024,256]{2,1,0:T(8,128)(2,1)} %param.11) | copy-start | bytes 1572868
  130.6 1.5 copy-start.1
  146.6 14.7 %copy-start.21 = (bf16[128,2560]{1,0:T(8,128)(2,1)S(1)}, bf16[128,2560]{1,0:T(8,128)(2,1)}, u32[]{:S(2)}) copy-start(bf16[128,2560]{1,0:T(8,128)(2,1)} %reduce-scatter.2.cloned.1.call-done) | copy-start | bytes 1966084
  146.6 14.6 %collective-permute-start.9 = (bf16[64,2560]{1,0:T(8,128)(2,1)S(1)}, bf16[64,2560]{1,0:T(8,128)(2,1)S(1)}, u32[]{:S(2)}, u32[]{:S(2)}) collective-permute-start(bf16[64,2560]{1,0:T(8,128)(2,1)S(1)} %slice.15), channel_id=1, source_target_pairs={{0,8},{1,9},{2,10},{3,11},{4,12},{5,13},{6,14},{7,15},{8,0},{9,1},... | collective-permute-start | bytes 983048 | tf_op jit(solution)/shard_map/ppermute | solution.py:361
Sparse Core Ops, SparseCore 0:
  9.8 47.5 all-gather.1
  75.2 70.4 reduce-scatter.1
